TPU v7x, 512 devices: a whole 4x8x8 slice. The times are simulated.
512 devices in a mesh: blk: 64 (over z_hi, y, core), group: 8 (over z_lo, x).
Axes of the slice: x: 4, y: 8, z: 8 (z_hi: 4, z_lo: 2; z = z_hi * 2 + z_lo), core: 2. Of those that a mesh axis runs over, the one named last changes fastest.
Arguments:
- image_rows: bfloat16 [65536, 768], P(('blk', 'group')), may hold values from -0.59765625 to 0.59765625
- text_rows: bfloat16 [65536, 768], P(('blk', 'group')), may hold values from -0.59765625 to 0.59765625
- log_norm: float32 [65536], P(('blk', 'group'))
- row_grad: float32 [65536], P(('blk', 'group')), may hold values from 0.25 to 2
- pos_index: int32 [65536], P(('blk', 'group')), may hold values from 0 to 1023
- logit_scale: float32 [], replicated, may hold values from 10 to 16
Outputs:
- image_grad: bfloat16 [65536, 768], P(('blk', 'group'))
- text_grad: bfloat16 [65536, 768], P(('blk', 'group'))
Inputs may be any that keep to these rules, and one draw needn't show every extreme that they name: `pos_index`: the positive text lies in the image row's own block.
All inputs are finite; a program needn't handle non-finite values.
Results may differ from a plain program's by a relative error of at most 0.015.
Values may be sent and summed in bfloat16 or wider, within the bound.
A program may use at most 64 MiB of HBM per device.

v0:
```python
import jax
import jax.numpy as jnp
from jax import lax
from jax.sharding import PartitionSpec as P

WINDOW = 4


def from_behind(value, axis, steps):
    count = lax.axis_size(axis)
    pairs = [(source, (source + steps) % count) for source in range(count)]
    return lax.ppermute(value, axis, pairs)


def weigh_rows(image_part, text_part, log_part, grad_part, pos_part, logit_scale, with_pos):
    scores = lax.dot_general(
        image_part, text_part, (((1,), (1,)), ((), ())), preferred_element_type=jnp.float32
    )
    row_prob = jnp.exp(logit_scale * scores - log_part[:, None])
    if with_pos:
        column = lax.broadcasted_iota(jnp.int32, row_prob.shape, 1)
        row_prob = row_prob - (column == pos_part[:, None]).astype(jnp.float32)
    return (row_prob * (logit_scale * grad_part)[:, None]).astype(jnp.bfloat16)


def text_term_of(weight, image_part):
    return lax.dot_general(
        weight, image_part, (((0,), (0,)), ((), ())), preferred_element_type=jnp.float32
    )


def add_term(partial_value, text_term, first):
    if first:
        return text_term.astype(jnp.bfloat16)
    return (partial_value.astype(jnp.float32) + text_term).astype(jnp.bfloat16)


def per_device(image_rows, text_rows, log_norm, row_grad, pos_index, logit_scale):
    text_block = lax.all_gather(text_rows, "group", axis=0, tiled=True)
    partial_value = None
    moving = text_block
    image_total = jnp.zeros(image_rows.shape, jnp.float32)
    for cycle_step in range(WINDOW):
        weight = weigh_rows(
            image_rows, moving, log_norm, row_grad, pos_index, logit_scale, cycle_step == 0
        )
        image_total = image_total + jnp.dot(weight, moving, preferred_element_type=jnp.float32)
        partial_value = add_term(partial_value, text_term_of(weight, image_rows), cycle_step == 0)
        if cycle_step + 1 < WINDOW:
            moving, partial_value = from_behind((moving, partial_value), "blk", 1)
    partial_value = from_behind(partial_value, "blk", 1 - WINDOW)
    image_grad = image_total.astype(jnp.bfloat16)
    text_grad = lax.psum_scatter(
        partial_value.astype(jnp.float32).astype(jnp.bfloat16),
        "group",
        scatter_dimension=0,
        tiled=True,
    )
    return (image_grad, text_grad)


def solution(mesh):
    return jax.shard_map(
        per_device,
        mesh=mesh,
        in_specs=(
            P(("blk", "group"), None),
            P(("blk", "group"), None),
            P(("blk", "group")),
            P(("blk", "group")),
            P(("blk", "group")),
            P(),
        ),
        out_specs=(P(("blk", "group"), None), P(("blk", "group"), None)),
        check_vma=False,
    )
```

profile of v0, /device:TPU:1, one launch (start us, length us, event | category | flops | bytes accessed | tf_op | source)
XLA Modules:
  0.0 355.9 jit_solution(14194385779773856226)
XLA Ops:
  7.2 0.0 copy-start
  7.2 0.0 all-gather.2.cloned.1.call-start
  7.2 0.7 all-gather.2.cloned.1.call-update
  7.9 0.0 reduce-scatter.2.cloned.1.call-start
  8.6 0.7 broadcast_multiply_fusion
  9.3 46.2 %all-gather.2.cloned.1.call-done = bf16[1024,768]{1,0:T(8,128)(2,1)} async-done(((bf16[128,768]{1,0:T(8,128)(2,1)}), bf16[1024,768]{1,0:T(8,128)(2,1)}) %all-gather.2.cloned.1.call-update) | async-done | bytes 1572880 | tf_op jit(solution)/shard_map/all_gather | solution.py:39
  55.5 9.8 %collective-permute-start = (bf16[1024,768]{1,0:T(8,128)(2,1)}, bf16[1024,768]{1,0:T(8,128)(2,1)S(1)}, u32[]{:S(2)}, u32[]{:S(2)}) collective-permute-start(bf16[1024,768]{1,0:T(8,128)(2,1)} %all-gather.2.cloned.1.call-done), channel_id=1, source_target_pairs={{0,8},{8,16},{16,24},{24,32},{32,40},{40,48},{48,56},{56,64},{64,7... | collective-permute-start | bytes 4718600 | tf_op jit(solution)/shard_map/ppermute | solution.py:12
  65.3 0.0 copy-done
  65.3 2.1 fusion.13
  67.4 0.0 copy-start.9
  67.4 0.0 copy-start.10
  67.4 0.6 convolution_convert_fusion
  68.0 1.9 collective-permute-start.3
  70.0 0.0 copy-done.9
  70.0 12.9 %collective-permute-done = bf16[1024,768]{1,0:T(8,128)(2,1)S(1)} collective-permute-done((bf16[1024,768]{1,0:T(8,128)(2,1)}, bf16[1024,768]{1,0:T(8,128)(2,1)S(1)}, u32[]{:S(2)}, u32[]{:S(2)}) %collective-permute-start) | collective-permute-done | bytes 1572896 | tf_op jit(solution)/shard_map/ppermute | solution.py:12
  82.9 4.3 %collective-permute-start.1 = (bf16[1024,768]{1,0:T(8,128)(2,1)S(1)}, bf16[1024,768]{1,0:T(8,128)(2,1)S(1)}, u32[]{:S(2)}, u32[]{:S(2)}) collective-permute-start(bf16[1024,768]{1,0:T(8,128)(2,1)S(1)} %collective-permute-done), channel_id=1, source_target_pairs={{0,8},{8,16},{16,24},{24,32},{32,40},{40,48},{48,56},{56,64},{64,7... | collective-permute-start | bytes 4718600 | tf_op jit(solution)/shard_map/ppermute | solution.py:12
  87.2 0.0 copy-done.10
  87.2 0.7 fusion.16
  87.9 0.0 copy-start.3
  87.9 11.8 %collective-permute-done.3 = bf16[1024,768]{1,0:T(8,128)(2,1)S(1)} collective-permute-done((bf16[1024,768]{1,0:T(8,128)(2,1)S(1)}, bf16[1024,768]{1,0:T(8,128)(2,1)S(1)}, u32[]{:S(2)}, u32[]{:S(2)}) %collective-permute-start.3) | collective-permute-done | bytes 1572896 | tf_op jit(solution)/shard_map/ppermute | solution.py:12
  99.7 0.6 add_convert_fusion.2
  100.3 4.4 %collective-permute-start.4 = (bf16[1024,768]{1,0:T(8,128)(2,1)S(1)}, bf16[1024,768]{1,0:T(8,128)(2,1)S(1)}, u32[]{:S(2)}, u32[]{:S(2)}) collective-permute-start(bf16[1024,768]{1,0:T(8,128)(2,1)S(1)} %add_convert_fusion.2), channel_id=1, source_target_pairs={{0,8},{8,16},{16,24},{24,32},{32,40},{40,48},{48,56},{56,64},{64,7... | collective-permute-start | bytes 4718600 | tf_op jit(solution)/shard_map/ppermute | solution.py:12
  104.7 11.8 %collective-permute-done.1 = bf16[1024,768]{1,0:T(8,128)(2,1)S(1)} collective-permute-done((bf16[1024,768]{1,0:T(8,128)(2,1)S(1)}, bf16[1024,768]{1,0:T(8,128)(2,1)S(1)}, u32[]{:S(2)}, u32[]{:S(2)}) %collective-permute-start.1) | collective-permute-done | bytes 1572896 | tf_op jit(solution)/shard_map/ppermute | solution.py:12
  116.5 4.4 %collective-permute-start.2 = (bf16[1024,768]{1,0:T(8,128)(2,1)S(1)}, bf16[1024,768]{1,0:T(8,128)(2,1)S(1)}, u32[]{:S(2)}, u32[]{:S(2)}) collective-permute-start(bf16[1024,768]{1,0:T(8,128)(2,1)S(1)} %collective-permute-done.1), channel_id=1, source_target_pairs={{0,8},{8,16},{16,24},{24,32},{32,40},{40,48},{48,56},{56,64},{64,7... | collective-permute-start | bytes 4718600 | tf_op jit(solution)/shard_map/ppermute | solution.py:12
  120.9 0.7 fusion.15
  121.6 0.6 fusion.19
  122.2 0.1 copy-done.5
  122.3 23.1 %collective-permute-done.4 = bf16[1024,768]{1,0:T(8,128)(2,1)S(1)} collective-permute-done((bf16[1024,768]{1,0:T(8,128)(2,1)S(1)}, bf16[1024,768]{1,0:T(8,128)(2,1)S(1)}, u32[]{:S(2)}, u32[]{:S(2)}) %collective-permute-start.4) | collective-permute-done | bytes 1572896 | tf_op jit(solution)/shard_map/ppermute | solution.py:12
  145.4 0.4 add_convert_fusion.1
  145.8 1.9 collective-permute-start.5
  147.7 31.2 %collective-permute-done.2 = bf16[1024,768]{1,0:T(8,128)(2,1)S(1)} collective-permute-done((bf16[1024,768]{1,0:T(8,128)(2,1)S(1)}, bf16[1024,768]{1,0:T(8,128)(2,1)S(1)}, u32[]{:S(2)}, u32[]{:S(2)}) %collective-permute-start.2) | collective-permute-done | bytes 1572896 | tf_op jit(solution)/shard_map/ppermute | solution.py:12
  178.9 0.7 fusion.14
  179.6 0.6 fusion.20
  180.2 0.0 copy-done.1
  180.2 0.1 copy-done.7
  180.3 33.1 %collective-permute-done.5 = bf16[1024,768]{1,0:T(8,128)(2,1)S(1)} collective-permute-done((bf16[1024,768]{1,0:T(8,128)(2,1)S(1)}, bf16[1024,768]{1,0:T(8,128)(2,1)S(1)}, u32[]{:S(2)}, u32[]{:S(2)}) %collective-permute-start.5) | collective-permute-done | bytes 1572896 | tf_op jit(solution)/shard_map/ppermute | solution.py:12
  213.4 0.4 add_convert_fusion
  213.8 1.9 collective-permute-start.6
  215.7 30.5 %collective-permute-done.6 = bf16[1024,768]{1,0:T(8,128)(2,1)} collective-permute-done((bf16[1024,768]{1,0:T(8,128)(2,1)S(1)}, bf16[1024,768]{1,0:T(8,128)(2,1)}, u32[]{:S(2)}, u32[]{:S(2)}) %collective-permute-start.6) | collective-permute-done | bytes 1572896 | tf_op jit(solution)/shard_map/ppermute | solution.py:12
  246.2 0.0 reduce-scatter.2.cloned.1.call-update
  246.2 1.9 fusion.18
  248.2 0.4 convolution_add_fusion.2
  248.6 0.5 copy-done.6
  249.1 0.4 convolution_add_fusion.1
  249.5 1.0 copy-done.2
  250.5 0.0 copy-done.8
  250.5 1.1 fusion.17
  251.6 97.5 %reduce-scatter.2.cloned.1.call-done = bf16[128,768]{1,0:T(8,128)(2,1)} async-done(((bf16[1024,768]{1,0:T(8,128)(2,1)}), bf16[128,768]{1,0:T(8,128)(2,1)}) %reduce-scatter.2.cloned.1.call-update) | async-done | bytes 196624 | tf_op jit(solution)/shard_map/reduce_scatter | solution.py:53
  (9 shorter events, 0.0 us)
Async XLA Ops:
  7.2 58.1 %copy-start = (bf16[128,768]{1,0:T(8,128)(2,1)S(1)}, bf16[128,768]{1,0:T(8,128)(2,1)}, u32[]{:S(2)}) copy-start(bf16[128,768]{1,0:T(8,128)(2,1)} %param.6) | copy-start | bytes 589828
  7.2 48.3 %all-gather.2.cloned.1.call-start = ((), (), s32[]{:S(2)}) async-start(), calls=%async_computation.1 | async-start | bytes 1769472 | tf_op jit(solution)/shard_map/all_gather | solution.py:39
  7.9 341.2 %reduce-scatter.2.cloned.1.call-start = ((), (), s32[]{:S(2)}) async-start(), calls=%async_computation.2 | async-start | bytes 1769472 | tf_op jit(solution)/shard_map/reduce_scatter | solution.py:53
  55.5 27.5 %collective-permute-start = (bf16[1024,768]{1,0:T(8,128)(2,1)}, bf16[1024,768]{1,0:T(8,128)(2,1)S(1)}, u32[]{:S(2)}, u32[]{:S(2)}) collective-permute-start(bf16[1024,768]{1,0:T(8,128)(2,1)} %all-gather.2.cloned.1.call-done), channel_id=1, source_target_pairs={{0,8},{8,16},{16,24},{24,32},{32,40},{40,48},{48,56},{56,64},{64,7... | collective-permute-start | bytes 4718600 | tf_op jit(solution)/shard_map/ppermute | solution.py:12
  67.4 2.6 copy-start.9
  67.4 19.8 %copy-start.10 = (f32[128]{0:T(128)S(1)}, f32[128]{0:T(128)}, u32[]{:S(2)}) copy-start(f32[128]{0:T(128)} %param.8) | copy-start | bytes 1540
  68.0 31.6 %collective-permute-start.3 = (bf16[1024,768]{1,0:T(8,128)(2,1)S(1)}, bf16[1024,768]{1,0:T(8,128)(2,1)S(1)}, u32[]{:S(2)}, u32[]{:S(2)}) collective-permute-start(bf16[1024,768]{1,0:T(8,128)(2,1)S(1)} %convolution_convert_fusion), channel_id=1, source_target_pairs={{0,8},{8,16},{16,24},{24,32},{32,40},{40,48},{48,56},{56,64},{64,7... | collective-permute-start | bytes 4718600 | tf_op jit(solution)/shard_map/ppermute | solution.py:12
  82.9 33.6 %collective-permute-start.1 = (bf16[1024,768]{1,0:T(8,128)(2,1)S(1)}, bf16[1024,768]{1,0:T(8,128)(2,1)S(1)}, u32[]{:S(2)}, u32[]{:S(2)}) collective-permute-start(bf16[1024,768]{1,0:T(8,128)(2,1)S(1)} %collective-permute-done), channel_id=1, source_target_pairs={{0,8},{8,16},{16,24},{24,32},{32,40},{40,48},{48,56},{56,64},{64,7... | collective-permute-start | bytes 4718600 | tf_op jit(solution)/shard_map/ppermute | solution.py:12
  87.9 12.4 %copy-start.3 = (bf16[128,1024]{1,0:T(8,128)(2,1)}, bf16[128,1024]{1,0:T(8,128)(2,1)S(1)}, u32[]{:S(2)}) copy-start(bf16[128,1024]{1,0:T(8,128)(2,1)S(1)} %fusion.16) | copy-start | bytes 786436
  100.3 45.1 %collective-permute-start.4 = (bf16[1024,768]{1,0:T(8,128)(2,1)S(1)}, bf16[1024,768]{1,0:T(8,128)(2,1)S(1)}, u32[]{:S(2)}, u32[]{:S(2)}) collective-permute-start(bf16[1024,768]{1,0:T(8,128)(2,1)S(1)} %add_convert_fusion.2), channel_id=1, source_target_pairs={{0,8},{8,16},{16,24},{24,32},{32,40},{40,48},{48,56},{56,64},{64,7... | collective-permute-start | bytes 4718600 | tf_op jit(solution)/shard_map/ppermute | solution.py:12
  116.5 62.4 %collective-permute-start.2 = (bf16[1024,768]{1,0:T(8,128)(2,1)S(1)}, bf16[1024,768]{1,0:T(8,128)(2,1)S(1)}, u32[]{:S(2)}, u32[]{:S(2)}) collective-permute-start(bf16[1024,768]{1,0:T(8,128)(2,1)S(1)} %collective-permute-done.1), channel_id=1, source_target_pairs={{0,8},{8,16},{16,24},{24,32},{32,40},{40,48},{48,56},{56,64},{64,7... | collective-permute-start | bytes 4718600 | tf_op jit(solution)/shard_map/ppermute | solution.py:12
  121.6 0.7 copy-start.5
  145.8 67.6 %collective-permute-start.5 = (bf16[1024,768]{1,0:T(8,128)(2,1)S(1)}, bf16[1024,768]{1,0:T(8,128)(2,1)S(1)}, u32[]{:S(2)}, u32[]{:S(2)}) collective-permute-start(bf16[1024,768]{1,0:T(8,128)(2,1)S(1)} %add_convert_fusion.1), channel_id=1, source_target_pairs={{0,8},{8,16},{16,24},{24,32},{32,40},{40,48},{48,56},{56,64},{64,7... | collective-permute-start | bytes 4718600 | tf_op jit(solution)/shard_map/ppermute | solution.py:12
  178.9 1.3 copy-start.1
  179.6 0.7 copy-start.7
  213.8 32.4 %collective-permute-start.6 = (bf16[1024,768]{1,0:T(8,128)(2,1)S(1)}, bf16[1024,768]{1,0:T(8,128)(2,1)}, u32[]{:S(2)}, u32[]{:S(2)}) collective-permute-start(bf16[1024,768]{1,0:T(8,128)(2,1)S(1)} %add_convert_fusion), channel_id=1, source_target_pairs={{0,488},{8,496},{16,504},{24,0},{32,8},{40,16},{48,24},{56,32},{64... | collective-permute-start | bytes 4718600 | tf_op jit(solution)/shard_map/ppermute | solution.py:12
  246.2 1.9 copy-start.4
  248.2 1.0 copy-start.6
  249.1 1.4 copy-start.2
  249.1 1.4 copy-start.8
Sparse Core Ops, SparseCore 0:
  10.1 45.3 all-gather.1
  246.3 102.6 reduce-scatter.1
where the time goes:
time: 361 us; the launch traced here: 356 us
  waiting for transfers between devices  299 us (83%)
  starting transfers between devices  28.7 us (8%)
  between operations  14.9 us (4%)
  matrix products  10.3 us (3%)
    ppermute x7, waiting for transfers between devices, from_behind(): return lax.ppermute(value, axis, pairs)  154 us
    reduce_scatter x1, waiting for transfers between devices, per_device(): lax.psum_scatter(partial_value.astype(jnp.float32).astype(jnp.bfloat16),...  97.5 us
    all_gather x1, waiting for transfers between devices, per_device(): text_block = lax.all_gather(text_rows, 'group', axis=0, tiled=True)  46.2 us
    ppermute x7, starting transfers between devices, from_behind(): return lax.ppermute(value, axis, pairs)  28.6 us
  transfers between devices with their start and end apart: 9, of which 9 were waited for; matrix products, arithmetic and copies ran while one was open for 3% of the time, Pallas kernels for 0%

commit v1 on v0

v1 whole, which is shorter than its diff:
```python
import functools

import jax
import jax.numpy as jnp
from jax import lax
from jax.experimental import pallas as pl
from jax.experimental.pallas import tpu as pltpu
from jax.sharding import PartitionSpec as P

MESH = pl.DeviceIdType.MESH
WINDOW = 4
F32 = jnp.float32
BF16 = jnp.bfloat16

(T_NEXT, T_FAR, T_SIDE, T_CORE, T_CORE_SIDE, T_PASS, T_PASS_SIDE, T_HOP, T_HOP_FAR) = range(9)
IMG = 9
PRM = 12
(G_CORE, G_CORE_OWN, G_SIDE_OWN, G_SIDE_BACK, G_SIDE_FAR, G_BACK, G_FAR) = range(15, 22)
IGR = 22
N_COPIES = 25


def kernel(n_blk, scale_ref, image_ref, text_ref, log_ref, grad_ref, pos_ref, image_out, text_out,
           img, prm, tx, rowv, posv, w, tg, ig, core_out, core_in, side_out, side_in, far_out, far_in,
           img_out, img_in, load_sem, send_sem, recv_sem):
    rows = image_ref.shape[0]
    blk, grp = lax.axis_index("blk"), lax.axis_index("group")
    c = blk % 2
    pair = blk // 2
    n_pair = n_blk // 2
    z, x = grp // 4, grp % 4
    x_a = x + 1 - 2 * (x % 2)
    x_b = 3 - x

    def at_pair(step, core):
        return ((pair + step + n_pair) % n_pair) * 2 + core

    core_dev = (pair * 2 + 1 - c, grp)
    side_dev = (blk, z * 4 + x_b)
    img_devs = ((blk, z * 4 + x_a), (blk, (1 - z) * 4 + x), (blk, (1 - z) * 4 + x_a))
    next_dev = (at_pair(1, c), grp)
    back_dev = (at_pair(-1, c), grp)
    far_dev = (at_pair(4 * c - 2, 1 - c), grp)

    own, side = pl.ds(0, rows), pl.ds(rows, rows)

    def copy(index, src, dst, device):
        return pltpu.make_async_remote_copy(
            src_ref=src, dst_ref=dst, send_sem=send_sem.at[index], recv_sem=recv_sem.at[index],
            device_id=device, device_id_type=MESH,
        )

    loads = [
        pltpu.make_async_copy(text_ref, tx.at[0, own], load_sem.at[0]),
        pltpu.make_async_copy(image_ref, img.at[own], load_sem.at[1]),
        pltpu.make_async_copy(log_ref, rowv.at[0], load_sem.at[2]),
        pltpu.make_async_copy(grad_ref, rowv.at[1], load_sem.at[3]),
        pltpu.make_async_copy(pos_ref, posv, load_sem.at[4]),
    ]
    for load in loads:
        load.start()

    barrier = pltpu.get_barrier_semaphore()
    partners = (core_dev, side_dev, *img_devs, next_dev, back_dev, far_dev)
    for device in partners:
        pl.semaphore_signal(barrier, inc=1, device_id=device, device_id_type=MESH)
    for load in loads:
        load.wait()
    prm[0:1, 0:rows] = rowv[0]
    prm[1:2, 0:rows] = rowv[1]
    prm[2:3, 0:rows] = posv[...].astype(F32)
    prm[3:8, 0:rows] = jnp.zeros((5, rows), F32)
    pl.semaphore_wait(barrier, len(partners))

    scale = scale_ref[0, 0]
    base_own = (grp * rows).astype(F32)
    base_side = ((z * 4 + x_b) * rows).astype(F32)

    t_next = copy(T_NEXT, tx.at[0, own], tx.at[2, own], next_dev)
    t_far = copy(T_FAR, tx.at[0, own], tx.at[3, own], far_dev)
    t_side = copy(T_SIDE, tx.at[0, own], tx.at[0, side], side_dev)
    t_core = copy(T_CORE, tx.at[0, own], tx.at[1, own], core_dev)
    t_core_side = copy(T_CORE_SIDE, tx.at[0, side], tx.at[1, side], core_dev)
    pass_slot = 3 - 2 * c
    get_slot = 1 + 2 * c
    t_pass = copy(T_PASS, tx.at[2, own], tx.at[pass_slot, own], core_dev)
    t_pass_side = copy(T_PASS_SIDE, tx.at[2, side], tx.at[pass_slot, side], core_dev)
    t_hop = copy(T_HOP, tx.at[2, own], tx.at[2, side], side_dev)
    t_hop_far = copy(T_HOP_FAR, tx.at[3, own], tx.at[3, side], side_dev)
    images = [copy(IMG + i, img.at[own], img.at[pl.ds((i + 1) * rows, rows)], img_devs[i]) for i in range(3)]
    params = [copy(PRM + i, prm.at[:, own], prm.at[:, pl.ds((i + 1) * rows, rows)], img_devs[i]) for i in range(3)]
    g_core = copy(G_CORE, core_out.at[0], core_in.at[0], core_dev)
    g_core_own = copy(G_CORE_OWN, core_out.at[1], core_in.at[1], core_dev)
    g_side_own = copy(G_SIDE_OWN, side_out.at[0], side_in.at[0], side_dev)
    g_side_back = copy(G_SIDE_BACK, side_out.at[1], side_in.at[1], side_dev)
    g_side_far = copy(G_SIDE_FAR, side_out.at[2], side_in.at[2], side_dev)
    g_back = copy(G_BACK, far_out.at[0], far_in.at[0], back_dev)
    g_far = copy(G_FAR, far_out.at[1], far_in.at[1], far_dev)
    image_back = [copy(IGR + i, img_out.at[i], img_in.at[i], img_devs[i]) for i in range(3)]

    t_next.start()
    pl.when(c == 1)(t_far.start)
    t_side.start()
    pl.when(c == 0)(t_core.start)
    for i in (2, 0, 1):
        images[i].start()
        params[i].start()

    t_side.wait_recv()
    pl.when(c == 0)(t_core_side.start)
    t_next.wait_recv()
    t_hop.start()
    t_pass.start()

    @pl.when(c == 0)
    def _():
        t_far.wait_recv()
        t_hop_far.start()

    for i in range(3):
        params[i].wait_recv()
        images[i].wait_recv()

    def step_body(s, _):
        later = 1 + s % 3
        k = c * s + (1 - c) * ((s + 2) // 3) * later

        @pl.when((s == 1) & (c == 0))
        def _():
            t_hop.wait_recv()
            t_pass_side.start()

        @pl.when((s == 2) & (c == 0))
        def _():
            t_hop_far.wait_recv()

        @pl.when((s == 1) & (c == 1))
        def _():
            t_core.wait_recv()
            t_core_side.wait_recv()

        @pl.when((s == 2) & (c == 1))
        def _():
            t_hop.wait_recv()
            t_pass_side.start()

        @pl.when(s == 3)
        def _():
            t_pass.wait_recv()
            t_pass_side.wait_recv()

        text = tx[k]
        scores = lax.dot_general(text, img[...], (((1,), (1,)), ((), ())), preferred_element_type=F32)
        prob = jnp.exp(scale * scores - prm[0:1, :])
        row = lax.broadcasted_iota(jnp.int32, scores.shape, 0)
        place = jnp.where(row < rows, row.astype(F32) + base_own, (row - rows).astype(F32) + base_side)
        place = place + (k * 65536).astype(F32)
        prob = prob - jnp.where(place == prm[2:3, :], 1.0, 0.0)
        w[...] = (prob * (scale * prm[1:2, :])).astype(BF16)
        tg[k] = jnp.dot(w[...], img[...], preferred_element_type=F32)

        @pl.when((s == 0) & (c == 1))
        def _():
            side_out[0] = tg[0, side].astype(BF16)
            g_side_own.start()

        @pl.when((s == 1) & (c == 1))
        def _():
            core_out[1] = tg[1].astype(BF16)
            g_core_own.start()

        @pl.when((s == 2) & (c == 0))
        def _():
            side_out[2] = tg[3, side].astype(BF16)
            g_side_far.start()

        @pl.when(s == 3)
        def _():
            core_out[0] = tg[k].astype(BF16)
            g_core.start()

        term = lax.dot_general(w[...], tx[k], (((0,), (0,)), ((), ())), preferred_element_type=F32)

        @pl.when(s == 0)
        def _():
            ig[...] = term

        @pl.when(s > 0)
        def _():
            ig[...] += term

        return 0

    lax.fori_loop(0, WINDOW, step_body, 0)

    for i in (2, 0, 1):
        img_out[i] = ig[(i + 1) * rows:(i + 2) * rows].astype(BF16)
        image_back[i].start()

    g_core.wait_recv()
    side_out[1] = (tg[2, side] + core_in[0, side].astype(F32)).astype(BF16)
    g_side_back.start()

    @pl.when(c == 0)
    def _():
        g_core_own.wait_recv()
        side_out[0] = (tg[0, side] + core_in[1, side].astype(F32)).astype(BF16)
        g_side_own.start()
        tg[0, own] += core_in[1, own].astype(F32)
        g_side_far.wait_recv()
        far_out[1] = (tg[3, own] + side_in[2].astype(F32)).astype(BF16)
        g_far.start()

    tg[2, own] += core_in[0, own].astype(F32)
    g_side_back.wait_recv()
    far_out[0] = (tg[2, own] + side_in[1].astype(F32)).astype(BF16)
    g_back.start()
    g_side_own.wait_recv()
    tg[0, own] += side_in[0].astype(F32)

    for i in range(3):
        image_back[i].wait_recv()
    image_out[...] = (
        (ig[own] + img_in[0].astype(F32)) + (img_in[1].astype(F32) + img_in[2].astype(F32))
    ).astype(BF16)

    g_back.wait_recv()

    @pl.when(c == 1)
    def _():
        g_far.wait_recv()
        tg[0, own] += far_in[1].astype(F32)

    text_out[...] = (tg[0, own] + far_in[0].astype(F32)).astype(BF16)

    for sent in (t_next, t_side, t_pass, t_pass_side, t_hop, *images, *params, g_core, g_side_own,
                 g_side_back, g_back, *image_back):
        sent.wait_send()

    @pl.when(c == 0)
    def _():
        for sent in (t_core, t_core_side, t_hop_far, g_side_far, g_far):
            sent.wait_send()

    @pl.when(c == 1)
    def _():
        for sent in (t_far, g_core_own):
            sent.wait_send()


def solution(mesh):
    n_blk = mesh.shape["blk"]

    def per_device(image_rows, text_rows, log_norm, row_grad, pos_index, logit_scale):
        rows, width = image_rows.shape
        block = pltpu.VMEM((rows, width), BF16)
        anywhere = pl.BlockSpec(memory_space=pl.ANY)
        return pl.pallas_call(
            functools.partial(kernel, n_blk),
            out_shape=(jax.ShapeDtypeStruct((rows, width), BF16),) * 2,
            in_specs=[pl.BlockSpec(memory_space=pltpu.SMEM)] + [anywhere] * 5,
            out_specs=(pl.BlockSpec(memory_space=pltpu.VMEM),) * 2,
            scratch_shapes=[
                pltpu.VMEM((4 * rows, width), BF16),
                pltpu.VMEM((8, 4 * rows), F32),
                pltpu.VMEM((WINDOW, 2 * rows, width), BF16),
                pltpu.VMEM((2, 1, rows), F32),
                pltpu.VMEM((1, rows), jnp.int32),
                pltpu.VMEM((2 * rows, 4 * rows), BF16),
                pltpu.VMEM((WINDOW, 2 * rows, width), F32),
                pltpu.VMEM((4 * rows, width), F32),
                pltpu.VMEM((2, 2 * rows, width), BF16),
                pltpu.VMEM((2, 2 * rows, width), BF16),
                pltpu.VMEM((3, rows, width), BF16),
                pltpu.VMEM((3, rows, width), BF16),
                pltpu.VMEM((2, rows, width), BF16),
                pltpu.VMEM((2, rows, width), BF16),
                pltpu.VMEM((3, rows, width), BF16),
                pltpu.VMEM((3, rows, width), BF16),
                pltpu.SemaphoreType.DMA((5,)),
                pltpu.SemaphoreType.DMA((N_COPIES,)),
                pltpu.SemaphoreType.DMA((N_COPIES,)),
            ],
            compiler_params=pltpu.CompilerParams(
                collective_id=0, has_side_effects=True, vmem_limit_bytes=40 * 2**20
            ),
            name="window_loss_grad",
        )(
            logit_scale.reshape(1, 1), image_rows, text_rows, log_norm.reshape(1, rows),
            row_grad.reshape(1, rows), pos_index.reshape(1, rows),
        )

    return jax.shard_map(
        per_device,
        mesh=mesh,
        in_specs=(
            P(("blk", "group"), None),
            P(("blk", "group"), None),
            P(("blk", "group")),
            P(("blk", "group")),
            P(("blk", "group")),
            P(),
        ),
        out_specs=(P(("blk", "group"), None), P(("blk", "group"), None)),
        check_vma=False,
    )
```

time: 361 us -> 61.4 us (0.17)
  the two profiles are of different devices: /device:TPU:1 before, /device:TPU:186 now
where the time goes in v1:
time: 61.4 us; the launch traced here: 61.2 us
  Pallas kernels  56 us (91%)
  local copies, waits for them, and re-layouts  3.87 us (6%)
  between operations  1.31 us (2%)
    pallas_call x1, Pallas kernels, per_device(): pl.pallas_call(functools.partial(kernel, n_blk), out_shape=(jax.ShapeDtyp...  56 us
    unnamed x12, local copies, waits for them, and re-layouts  3.87 us

profile of v1, /device:TPU:186, one launch (start us, length us, event | category | flops | bytes accessed | tf_op | source)
XLA Modules:
  0.0 61.2 jit_solution(9126805749170456003)
XLA Ops:
  1.3 0.0 copy-start.2
  1.3 0.0 copy-start.3
  1.3 0.0 copy-start.4
  1.3 0.6 %copy-done.2 = f32[128]{0:T(128)S(1)} copy-done((f32[128]{0:T(128)S(1)}, f32[128]{0:T(128)}, u32[]{:S(2)}) %copy-start.2) | copy-done | bytes 536
  1.9 0.0 copy-done.3
  1.9 0.0 copy-done.4
  2.0 0.0 copy-start
  2.0 0.9 %copy-done = bf16[128,768]{1,0:T(8,128)(2,1)S(1)} copy-done((bf16[128,768]{1,0:T(8,128)(2,1)S(1)}, bf16[128,768]{1,0:T(8,128)(2,1)}, u32[]{:S(2)}) %copy-start) | copy-done | bytes 196632
  2.9 0.0 copy-start.1
  2.9 0.9 %copy-done.1 = bf16[128,768]{1,0:T(8,128)(2,1)S(1)} copy-done((bf16[128,768]{1,0:T(8,128)(2,1)S(1)}, bf16[128,768]{1,0:T(8,128)(2,1)}, u32[]{:S(2)}) %copy-start.1) | copy-done | bytes 196632
  3.8 56.0 %window_loss_grad.1 = (bf16[128,768]{1,0:T(8,128)(2,1)S(1)}, bf16[128,768]{1,0:T(8,128)(2,1)S(1)}) custom-call(f32[1,1]{1,0:T(1,128)} %bitcast.4.scale_ref, bf16[128,768]{1,0:T(8,128)(2,1)S(1)} %copy-done, bf16[128,768]{1,0:T(8,128)(2,1)S(1)} %copy-done.1, f32[1,128]{1,0:T(1,128)S(1)} %bitcast.5, f32[1,128]{1,0:T(1,128)S(1)} %bitcast.6, s32[1,128]{1,0:T(1,128)S(1)} %bitcast.7), custom_call_target="tpu_custom_call" | custom-call | tf_op jit(solution)/shard_map/window_loss_grad/pallas_call | solution.py:258
  59.8 0.7 %copy.11 = bf16[128,768]{1,0:T(8,128)(2,1)} copy(bf16[128,768]{1,0:T(8,128)(2,1)S(1)} %get-tuple-element.4) | data formatting | bytes 393216
  60.5 0.7 %copy.12 = bf16[128,768]{1,0:T(8,128)(2,1)} copy(bf16[128,768]{1,0:T(8,128)(2,1)S(1)} %get-tuple-element.5) | data formatting | bytes 393216
Async XLA Ops:
  1.3 0.7 %copy-start.2 = (f32[128]{0:T(128)S(1)}, f32[128]{0:T(128)}, u32[]{:S(2)}) copy-start(f32[128]{0:T(128)} %param.8) | copy-start | bytes 1540
  1.3 0.7 %copy-start.3 = (f32[128]{0:T(128)S(1)}, f32[128]{0:T(128)}, u32[]{:S(2)}) copy-start(f32[128]{0:T(128)} %param.9) | copy-start | bytes 1540
  1.3 0.7 %copy-start.4 = (s32[128]{0:T(128)S(1)}, s32[128]{0:T(128)}, u32[]{:S(2)}) copy-start(s32[128]{0:T(128)} %param.10) | copy-start | bytes 1540
  2.0 0.9 %copy-start = (bf16[128,768]{1,0:T(8,128)(2,1)S(1)}, bf16[128,768]{1,0:T(8,128)(2,1)}, u32[]{:S(2)}) copy-start(bf16[128,768]{1,0:T(8,128)(2,1)} %image_ref.1) | copy-start | bytes 589828
  2.9 0.9 %copy-start.1 = (bf16[128,768]{1,0:T(8,128)(2,1)S(1)}, bf16[128,768]{1,0:T(8,128)(2,1)}, u32[]{:S(2)}) copy-start(bf16[128,768]{1,0:T(8,128)(2,1)} %text_ref.1) | copy-start | bytes 589828

commit v2 on v0

v2 whole, which is shorter than its diff:
```python
import functools

import jax
import jax.numpy as jnp
from jax import lax
from jax.experimental import pallas as pl
from jax.experimental.pallas import tpu as pltpu
from jax.sharding import PartitionSpec as P

MESH = pl.DeviceIdType.MESH
F32 = jnp.float32
BF16 = jnp.bfloat16
PIECES = 2

T_SIDE = 0
T_NEXT = 1
T_HOP = T_NEXT + PIECES
T_FAR = T_HOP + PIECES
T_FAR_HOP = T_FAR + PIECES
IMG = T_FAR_HOP + PIECES
PRM = IMG + 3
IMG_CORE = PRM + 3
PRM_CORE = IMG_CORE + 4
G_SIDE = PRM_CORE + 1
G_HOP = G_SIDE + 1
G_BACK = G_HOP + PIECES
G_FAR_HOP = G_BACK + PIECES
G_FAR = G_FAR_HOP + PIECES
IG_CORE = G_FAR + PIECES
IG = IG_CORE + 4
N_COPIES = IG + 3


def kernel(n_blk, scale_ref, image_ref, text_ref, log_ref, grad_ref, pos_ref, image_out, text_out,
           img, prm, tx, rowv, posv, w, tg, ig, core_out, core_in, side_out, side_in, hop_out, hop_in,
           back_out, back_in, img_out, img_in, load_sem, send_sem, recv_sem):
    rows = image_ref.shape[0]
    piece = rows // PIECES
    blk, grp = lax.axis_index("blk"), lax.axis_index("group")
    c = blk % 2
    pair = blk // 2
    n_pair = n_blk // 2
    z, x = grp // 4, grp % 4
    x_a = x + 1 - 2 * (x % 2)
    x_b = 3 - x

    def at_pair(step):
        return (((pair + step + n_pair) % n_pair) * 2 + c, grp)

    core_dev = (pair * 2 + 1 - c, grp)
    side_dev = (blk, z * 4 + x_b)
    img_devs = ((blk, z * 4 + x_a), (blk, (1 - z) * 4 + x), (blk, (1 - z) * 4 + x_a))
    next_dev, back_dev = at_pair(1), at_pair(-1)
    next2_dev, back2_dev = at_pair(2), at_pair(-2)

    own, side = pl.ds(0, rows), pl.ds(rows, rows)

    def slot(i):
        return pl.ds(i * rows, rows)

    def part(i):
        return pl.ds(i * piece, piece)

    def side_part(i):
        return pl.ds(rows + i * piece, piece)

    def copy(index, src, dst, device):
        return pltpu.make_async_remote_copy(
            src_ref=src, dst_ref=dst, send_sem=send_sem.at[index], recv_sem=recv_sem.at[index],
            device_id=device, device_id_type=MESH,
        )

    loads = [
        pltpu.make_async_copy(text_ref, tx.at[0, own], load_sem.at[0]),
        pltpu.make_async_copy(image_ref, img.at[c, own], load_sem.at[1]),
        pltpu.make_async_copy(log_ref, rowv.at[0], load_sem.at[2]),
        pltpu.make_async_copy(grad_ref, rowv.at[1], load_sem.at[3]),
        pltpu.make_async_copy(pos_ref, posv, load_sem.at[4]),
    ]
    for load in loads:
        load.start()

    barrier = pltpu.get_barrier_semaphore()
    partners = (core_dev, side_dev, *img_devs, next_dev, back_dev, next2_dev, back2_dev)
    for device in partners:
        pl.semaphore_signal(barrier, inc=1, device_id=device, device_id_type=MESH)
    for load in loads:
        load.wait()
    prm[c, 0:1, 0:rows] = rowv[0]
    prm[c, 1:2, 0:rows] = rowv[1]
    prm[c, 2:3, 0:rows] = posv[...].astype(F32)
    prm[c, 3:8, 0:rows] = jnp.zeros((5, rows), F32)
    pl.semaphore_wait(barrier, len(partners))

    scale = scale_ref[0, 0]
    base_own = (grp * rows).astype(F32)
    base_side = ((z * 4 + x_b) * rows).astype(F32)
    two = range(PIECES)

    t_side = copy(T_SIDE, tx.at[0, own], tx.at[0, side], side_dev)
    t_next = [copy(T_NEXT + i, tx.at[0, part(i)], tx.at[1, part(i)], next_dev) for i in two]
    t_hop = [copy(T_HOP + i, tx.at[1, part(i)], tx.at[1, side_part(i)], side_dev) for i in two]
    t_far = [copy(T_FAR + i, tx.at[1, part(i)], tx.at[2, part(i)], next_dev) for i in two]
    t_far_hop = [copy(T_FAR_HOP + i, tx.at[2, part(i)], tx.at[2, side_part(i)], side_dev) for i in two]
    images = [copy(IMG + i, img.at[c, own], img.at[c, slot(i + 1)], img_devs[i]) for i in range(3)]
    params = [copy(PRM + i, prm.at[c, :, own], prm.at[c, :, slot(i + 1)], img_devs[i]) for i in range(3)]
    img_core = [copy(IMG_CORE + i, img.at[c, slot(i)], img.at[c, slot(i)], core_dev) for i in range(4)]
    prm_core = copy(PRM_CORE, prm.at[c], prm.at[c], core_dev)
    img_got = [copy(IMG_CORE + i, img.at[1 - c, slot(i)], img.at[1 - c, slot(i)], core_dev) for i in range(4)]
    prm_got = copy(PRM_CORE, prm.at[1 - c], prm.at[1 - c], core_dev)

    g_side = copy(G_SIDE, side_out, side_in, side_dev)
    g_hop = [copy(G_HOP + i, hop_out.at[0, part(i)], hop_in.at[0, part(i)], side_dev) for i in two]
    g_far_hop = [copy(G_FAR_HOP + i, hop_out.at[1, part(i)], hop_in.at[1, part(i)], side_dev) for i in two]
    g_back = [copy(G_BACK + i, back_out.at[0, part(i)], back_in.at[0, part(i)], back_dev) for i in two]
    g_far = [copy(G_FAR + i, back_out.at[1, part(i)], back_in.at[1, part(i)], back2_dev) for i in two]
    ig_core = [copy(IG_CORE + i, core_out.at[slot(i)], core_in.at[slot(i)], core_dev) for i in range(4)]
    ig_back = [copy(IG + i, img_out.at[i], img_in.at[i], img_devs[i]) for i in range(3)]

    for i in two:
        t_next[i].start()
    for i in (2, 0, 1):
        images[i].start()
        params[i].start()
    t_side.start()
    img_core[0].start()

    for i in two:
        t_next[i].wait_recv()
        pl.when(c == 1)(t_far[i].start)
        t_hop[i].start()
    for i in (0, 1, 2):
        images[i].wait_recv()
        img_core[i + 1].start()
        params[i].wait_recv()
    prm_core.start()

    @pl.when(c == 1)
    def _():
        for i in two:
            t_far[i].wait_recv()
            t_far_hop[i].start()

    t_side.wait_recv()

    def tile(s, _):
        j = (s + 1) // 2 - (s // 3) * (2 - 2 * c)
        i = c + (s // 2) * (1 - 2 * c)

        @pl.when(s == 1)
        def _():
            for q in two:
                t_hop[q].wait_recv()

        @pl.when(s == 2)
        def _():
            for q in range(4):
                img_got[q].wait_recv()
            prm_got.wait_recv()

        @pl.when((s == 3) & (c == 1))
        def _():
            for q in two:
                t_far_hop[q].wait_recv()

        scores = lax.dot_general(tx[j], img[i], (((1,), (1,)), ((), ())), preferred_element_type=F32)
        prob = jnp.exp(scale * scores - prm[i, 0:1, :])
        row = lax.broadcasted_iota(jnp.int32, scores.shape, 0)
        place = jnp.where(row < rows, row.astype(F32) + base_own, (row - rows).astype(F32) + base_side)
        place = place + (s * 65536).astype(F32)
        prob = prob - jnp.where(place == prm[i, 2:3, :], 1.0, 0.0)
        w[...] = (prob * (scale * prm[i, 1:2, :])).astype(BF16)
        term = jnp.dot(w[...], img[i], preferred_element_type=F32)
        fresh = (s < 2) | ((s == 3) & (c == 1))

        @pl.when(fresh)
        def _():
            tg[j] = term

        @pl.when(jnp.logical_not(fresh))
        def _():
            tg[j] += term

        @pl.when(((s == 0) & (c == 1)) | ((s == 3) & (c == 0)))
        def _():
            side_out[...] = tg[0, side].astype(BF16)
            g_side.start()

        @pl.when(s == 2)
        def _():
            for q in two:
                hop_out[0, part(q)] = tg[1, side_part(q)].astype(BF16)
                g_hop[q].start()

        @pl.when((s == 3) & (c == 1))
        def _():
            for q in two:
                hop_out[1, part(q)] = tg[2, side_part(q)].astype(BF16)
                g_far_hop[q].start()

        back = lax.dot_general(w[...], tx[j], (((0,), (0,)), ((), ())), preferred_element_type=F32)

        @pl.when(s % 2 == 0)
        def _():
            ig[i] = back

        @pl.when(s % 2 == 1)
        def _():
            ig[i] += back

        return 0

    lax.fori_loop(0, 4, tile, 0)

    for i in (3, 1, 2, 0):
        core_out[slot(i)] = ig[1 - c, slot(i)].astype(BF16)
        ig_core[i].start()

    for i in (3, 1, 2):
        ig_core[i].wait_recv()
        img_out[i - 1] = (ig[c, slot(i)] + core_in[slot(i)].astype(F32)).astype(BF16)
        ig_back[i - 1].start()

    for i in two:
        g_hop[i].wait_recv()
        back_out[0, part(i)] = (tg[1, part(i)] + hop_in[0, part(i)].astype(F32)).astype(BF16)
        g_back[i].start()

    @pl.when(c == 1)
    def _():
        for i in two:
            g_far_hop[i].wait_recv()
            back_out[1, part(i)] = (tg[2, part(i)] + hop_in[1, part(i)].astype(F32)).astype(BF16)
            g_far[i].start()

    ig_core[0].wait_recv()
    ig[c, own] += core_in[own].astype(F32)
    g_side.wait_recv()
    tg[0, own] += side_in[...].astype(F32)

    for i in range(3):
        ig_back[i].wait_recv()
    image_out[...] = (
        (ig[c, own] + img_in[0].astype(F32)) + (img_in[1].astype(F32) + img_in[2].astype(F32))
    ).astype(BF16)

    for i in two:
        g_back[i].wait_recv()

    @pl.when(c == 0)
    def _():
        text_out[...] = (tg[0, own] + back_in[0].astype(F32)).astype(BF16)

    @pl.when(c == 1)
    def _():
        for i in two:
            g_far[i].wait_recv()
        text_out[...] = ((tg[0, own] + back_in[0].astype(F32)) + back_in[1].astype(F32)).astype(BF16)

    for sent in (t_side, *t_next, *t_hop, *images, *params, *img_core, prm_core, g_side, *g_hop, *g_back,
                 *ig_core, *ig_back):
        sent.wait_send()

    @pl.when(c == 1)
    def _():
        for sent in (*t_far, *t_far_hop, *g_far_hop, *g_far):
            sent.wait_send()


def solution(mesh):
    n_blk = mesh.shape["blk"]

    def per_device(image_rows, text_rows, log_norm, row_grad, pos_index, logit_scale):
        rows, width = image_rows.shape
        anywhere = pl.BlockSpec(memory_space=pltpu.HBM)
        return pl.pallas_call(
            functools.partial(kernel, n_blk),
            out_shape=(jax.ShapeDtypeStruct((rows, width), BF16),) * 2,
            in_specs=[pl.BlockSpec(memory_space=pltpu.SMEM)] + [anywhere] * 5,
            out_specs=(pl.BlockSpec(memory_space=pltpu.VMEM),) * 2,
            scratch_shapes=[
                pltpu.VMEM((2, 4 * rows, width), BF16),
                pltpu.VMEM((2, 8, 4 * rows), F32),
                pltpu.VMEM((3, 2 * rows, width), BF16),
                pltpu.VMEM((2, 1, rows), F32),
                pltpu.VMEM((1, rows), jnp.int32),
                pltpu.VMEM((2 * rows, 4 * rows), BF16),
                pltpu.VMEM((3, 2 * rows, width), F32),
                pltpu.VMEM((2, 4 * rows, width), F32),
                pltpu.VMEM((4 * rows, width), BF16),
                pltpu.VMEM((4 * rows, width), BF16),
                pltpu.VMEM((rows, width), BF16),
                pltpu.VMEM((rows, width), BF16),
                pltpu.VMEM((2, rows, width), BF16),
                pltpu.VMEM((2, rows, width), BF16),
                pltpu.VMEM((2, rows, width), BF16),
                pltpu.VMEM((2, rows, width), BF16),
                pltpu.VMEM((3, rows, width), BF16),
                pltpu.VMEM((3, rows, width), BF16),
                pltpu.SemaphoreType.DMA((5,)),
                pltpu.SemaphoreType.DMA((N_COPIES,)),
                pltpu.SemaphoreType.DMA((N_COPIES,)),
            ],
            compiler_params=pltpu.CompilerParams(
                collective_id=0, has_side_effects=True, vmem_limit_bytes=40 * 2**20
            ),
            name="window_loss_grad",
        )(
            logit_scale.reshape(1, 1), image_rows, text_rows, log_norm.reshape(1, rows),
            row_grad.reshape(1, rows), pos_index.reshape(1, rows),
        )

    return jax.shard_map(
        per_device,
        mesh=mesh,
        in_specs=(
            P(("blk", "group"), None),
            P(("blk", "group"), None),
            P(("blk", "group")),
            P(("blk", "group")),
            P(("blk", "group")),
            P(),
        ),
        out_specs=(P(("blk", "group"), None), P(("blk", "group"), None)),
        check_vma=False,
    )
```

time: 361 us -> 57.7 us (0.16); the launches traced: 356 us -> 57.4 us
  waiting for transfers between devices: 299 us -> 0 us
  Pallas kernels: 0 us -> 52.2 us
  starting transfers between devices: 28.7 us -> 0 us
  between operations: 14.9 us -> 1.31 us
  matrix products: 10.3 us -> 0 us
    ppermute x7 -> x0, waiting for transfers between devices: 154 us -> none  [from_behind(): return lax.ppermute(value, axis, pairs)]
    reduce_scatter x1 -> x0, waiting for transfers between devices: 97.5 us -> none  [per_device(): lax.psum_scatter(partial_value.astype(jnp.float32).astype(jnp.bfloat16),...]
    pallas_call x0 -> x1, Pallas kernels: none -> 52.2 us  [per_device(): pl.pallas_call(functools.partial(kernel, n_blk), out_shape=(jax.ShapeDtyp...]
    all_gather x1 -> x0, waiting for transfers between devices: 46.2 us -> none  [per_device(): text_block = lax.all_gather(text_rows, 'group', axis=0, tiled=True)]
    ppermute x7 -> x0, starting transfers between devices: 28.6 us -> none  [from_behind(): return lax.ppermute(value, axis, pairs)]
    dot_general x12 -> x0, matrix products: 10.3 us -> none  [the longest x4 4.13 us: weigh_rows(): lax.dot_general(image_part, text_part, (((1,), (1,)), ((), ())), preferre...]
  transfers between devices with their start and end apart: 9 -> 0, of which waited for: 9 -> 0; matrix products, arithmetic and copies ran while one was open for 3% -> 0% of each run, Pallas kernels for 0% -> 0%
where the time goes in v2:
time: 57.7 us; the launch traced here: 57.4 us
  Pallas kernels  52.2 us (90%)
  local copies, waits for them, and re-layouts  3.87 us (7%)
  between operations  1.31 us (2%)
    pallas_call x1, Pallas kernels, per_device(): pl.pallas_call(functools.partial(kernel, n_blk), out_shape=(jax.ShapeDtyp...  52.2 us
    unnamed x12, local copies, waits for them, and re-layouts  3.87 us

profile of v2, /device:TPU:1, one launch (start us, length us, event | category | flops | bytes accessed | tf_op | source)
XLA Modules:
  0.0 57.4 jit_solution(13345844588536052248)
XLA Ops:
  1.3 0.0 copy-start.2
  1.3 0.0 copy-start.3
  1.3 0.0 copy-start.4
  1.3 0.6 %copy-done.2 = f32[128]{0:T(128)S(1)} copy-done((f32[128]{0:T(128)S(1)}, f32[128]{0:T(128)}, u32[]{:S(2)}) %copy-start.2) | copy-done | bytes 536
  1.9 0.0 copy-done.3
  1.9 0.0 copy-done.4
  2.0 0.0 copy-start
  2.0 0.9 %copy-done = bf16[128,768]{1,0:T(8,128)(2,1)S(1)} copy-done((bf16[128,768]{1,0:T(8,128)(2,1)S(1)}, bf16[128,768]{1,0:T(8,128)(2,1)}, u32[]{:S(2)}) %copy-start) | copy-done | bytes 196632
  2.9 0.0 copy-start.1
  2.9 0.9 %copy-done.1 = bf16[128,768]{1,0:T(8,128)(2,1)S(1)} copy-done((bf16[128,768]{1,0:T(8,128)(2,1)S(1)}, bf16[128,768]{1,0:T(8,128)(2,1)}, u32[]{:S(2)}) %copy-start.1) | copy-done | bytes 196632
  3.8 52.2 %window_loss_grad.1 = (bf16[128,768]{1,0:T(8,128)(2,1)S(1)}, bf16[128,768]{1,0:T(8,128)(2,1)S(1)}) custom-call(f32[1,1]{1,0:T(1,128)} %bitcast.4.scale_ref, bf16[128,768]{1,0:T(8,128)(2,1)S(1)} %copy-done, bf16[128,768]{1,0:T(8,128)(2,1)S(1)} %copy-done.1, f32[1,128]{1,0:T(1,128)S(1)} %bitcast.5, f32[1,128]{1,0:T(1,128)S(1)} %bitcast.6, s32[1,128]{1,0:T(1,128)S(1)} %bitcast.7), custom_call_target="tpu_custom_call" | custom-call | tf_op jit(solution)/shard_map/window_loss_grad/pallas_call | solution.py:276
  56.0 0.7 %copy.11 = bf16[128,768]{1,0:T(8,128)(2,1)} copy(bf16[128,768]{1,0:T(8,128)(2,1)S(1)} %get-tuple-element.4) | data formatting | bytes 393216
  56.7 0.7 %copy.12 = bf16[128,768]{1,0:T(8,128)(2,1)} copy(bf16[128,768]{1,0:T(8,128)(2,1)S(1)} %get-tuple-element.5) | data formatting | bytes 393216
Async XLA Ops:
  1.3 0.7 %copy-start.2 = (f32[128]{0:T(128)S(1)}, f32[128]{0:T(128)}, u32[]{:S(2)}) copy-start(f32[128]{0:T(128)} %param.8) | copy-start | bytes 1540
  1.3 0.7 %copy-start.3 = (f32[128]{0:T(128)S(1)}, f32[128]{0:T(128)}, u32[]{:S(2)}) copy-start(f32[128]{0:T(128)} %param.9) | copy-start | bytes 1540
  1.3 0.7 %copy-start.4 = (s32[128]{0:T(128)S(1)}, s32[128]{0:T(128)}, u32[]{:S(2)}) copy-start(s32[128]{0:T(128)} %param.10) | copy-start | bytes 1540
  2.0 0.9 %copy-start = (bf16[128,768]{1,0:T(8,128)(2,1)S(1)}, bf16[128,768]{1,0:T(8,128)(2,1)}, u32[]{:S(2)}) copy-start(bf16[128,768]{1,0:T(8,128)(2,1)} %image_ref.1) | copy-start | bytes 589828
  2.9 0.9 %copy-start.1 = (bf16[128,768]{1,0:T(8,128)(2,1)S(1)}, bf16[128,768]{1,0:T(8,128)(2,1)}, u32[]{:S(2)}) copy-start(bf16[128,768]{1,0:T(8,128)(2,1)} %text_ref.1) | copy-start | bytes 589828

commit v3 on v2

--- a/solution.py
+++ b/solution.py
@@ -11,6 +11,7 @@
 F32 = jnp.float32
 BF16 = jnp.bfloat16
 PIECES = 2
+Y = 8
 
 T_SIDE = 0
 T_NEXT = 1
@@ -18,7 +19,9 @@
 T_FAR = T_HOP + PIECES
 T_FAR_HOP = T_FAR + PIECES
 IMG = T_FAR_HOP + PIECES
-PRM = IMG + 3
+IMG_Z = IMG + 1
+IMG_AZ = IMG_Z + PIECES
+PRM = IMG_AZ + PIECES
 IMG_CORE = PRM + 3
 PRM_CORE = IMG_CORE + 4
 G_SIDE = PRM_CORE + 1
@@ -28,12 +31,14 @@
 G_FAR = G_FAR_HOP + PIECES
 IG_CORE = G_FAR + PIECES
 IG = IG_CORE + 4
-N_COPIES = IG + 3
+T_RELAY = IG + 3
+G_RELAY = T_RELAY + 1
+N_COPIES = G_RELAY + 1
 
 
 def kernel(n_blk, scale_ref, image_ref, text_ref, log_ref, grad_ref, pos_ref, image_out, text_out,
            img, prm, tx, rowv, posv, w, tg, ig, core_out, core_in, side_out, side_in, hop_out, hop_in,
-           back_out, back_in, img_out, img_in, load_sem, send_sem, recv_sem):
+           back_out, back_in, img_out, img_in, relay, load_sem, send_sem, recv_sem, ready):
     rows = image_ref.shape[0]
     piece = rows // PIECES
     blk, grp = lax.axis_index("blk"), lax.axis_index("group")
@@ -49,9 +54,14 @@
 
     core_dev = (pair * 2 + 1 - c, grp)
     side_dev = (blk, z * 4 + x_b)
-    img_devs = ((blk, z * 4 + x_a), (blk, (1 - z) * 4 + x), (blk, (1 - z) * 4 + x_a))
+    a_dev, z_dev = (blk, z * 4 + x_a), (blk, (1 - z) * 4 + x)
+    img_devs = (a_dev, z_dev, (blk, (1 - z) * 4 + x_a))
     next_dev, back_dev = at_pair(1), at_pair(-1)
-    next2_dev, back2_dev = at_pair(2), at_pair(-2)
+    back2_dev = at_pair(-2)
+    y = pair % Y
+    last, first = y == Y - 1, y == 0
+    z_next, z_back = at_pair(Y), at_pair(-Y)
+    y_next, y_back = at_pair((y + 1) % Y - y), at_pair((y + Y - 1) % Y - y)
 
     own, side = pl.ds(0, rows), pl.ds(rows, rows)
 
@@ -61,8 +71,11 @@
     def part(i):
         return pl.ds(i * piece, piece)
 
+    def slot_part(s, i):
+        return pl.ds(s * rows + i * piece, piece)
+
     def side_part(i):
-        return pl.ds(rows + i * piece, piece)
+        return slot_part(1, i)
 
     def copy(index, src, dst, device):
         return pltpu.make_async_remote_copy(
@@ -81,16 +94,30 @@
         load.start()
 
     barrier = pltpu.get_barrier_semaphore()
-    partners = (core_dev, side_dev, *img_devs, next_dev, back_dev, next2_dev, back2_dev)
-    for device in partners:
+    senders = (core_dev, side_dev, *img_devs, back_dev)
+    for device in senders:
         pl.semaphore_signal(barrier, inc=1, device_id=device, device_id_type=MESH)
+
+    @pl.when(last)
+    def _():
+        pl.semaphore_signal(barrier, inc=1, device_id=z_back, device_id_type=MESH)
+
+    @pl.when(first)
+    def _():
+        pl.semaphore_signal(barrier, inc=1, device_id=y_back, device_id_type=MESH)
+        pl.semaphore_signal(barrier, inc=1, device_id=z_back, device_id_type=MESH)
+
     for load in loads:
         load.wait()
     prm[c, 0:1, 0:rows] = rowv[0]
     prm[c, 1:2, 0:rows] = rowv[1]
     prm[c, 2:3, 0:rows] = posv[...].astype(F32)
     prm[c, 3:8, 0:rows] = jnp.zeros((5, rows), F32)
-    pl.semaphore_wait(barrier, len(partners))
+    pl.semaphore_wait(barrier, len(senders) + jnp.where(last, 2, jnp.where(first, 1, 0)))
+
+    @pl.when(first)
+    def _():
+        pl.semaphore_signal(ready, inc=1, device_id=z_next, device_id_type=MESH)
 
     scale = scale_ref[0, 0]
     base_own = (grp * rows).astype(F32)
@@ -99,10 +126,14 @@
 
     t_side = copy(T_SIDE, tx.at[0, own], tx.at[0, side], side_dev)
     t_next = [copy(T_NEXT + i, tx.at[0, part(i)], tx.at[1, part(i)], next_dev) for i in two]
+    t_relay = copy(T_RELAY, tx.at[0, part(PIECES - 1)], relay.at[0], z_next)
+    t_passed = copy(T_NEXT + PIECES - 1, relay.at[0], tx.at[1, part(PIECES - 1)], y_next)
     t_hop = [copy(T_HOP + i, tx.at[1, part(i)], tx.at[1, side_part(i)], side_dev) for i in two]
     t_far = [copy(T_FAR + i, tx.at[1, part(i)], tx.at[2, part(i)], next_dev) for i in two]
     t_far_hop = [copy(T_FAR_HOP + i, tx.at[2, part(i)], tx.at[2, side_part(i)], side_dev) for i in two]
-    images = [copy(IMG + i, img.at[c, own], img.at[c, slot(i + 1)], img_devs[i]) for i in range(3)]
+    img_a = copy(IMG, img.at[c, own], img.at[c, slot(1)], a_dev)
+    img_z = [copy(IMG_Z + i, img.at[c, part(i)], img.at[c, slot_part(2, i)], z_dev) for i in two]
+    img_az = [copy(IMG_AZ + i, img.at[c, slot_part(2, i)], img.at[c, slot_part(3, i)], a_dev) for i in two]
     params = [copy(PRM + i, prm.at[c, :, own], prm.at[c, :, slot(i + 1)], img_devs[i]) for i in range(3)]
     img_core = [copy(IMG_CORE + i, img.at[c, slot(i)], img.at[c, slot(i)], core_dev) for i in range(4)]
     prm_core = copy(PRM_CORE, prm.at[c], prm.at[c], core_dev)
@@ -113,25 +144,46 @@
     g_hop = [copy(G_HOP + i, hop_out.at[0, part(i)], hop_in.at[0, part(i)], side_dev) for i in two]
     g_far_hop = [copy(G_FAR_HOP + i, hop_out.at[1, part(i)], hop_in.at[1, part(i)], side_dev) for i in two]
     g_back = [copy(G_BACK + i, back_out.at[0, part(i)], back_in.at[0, part(i)], back_dev) for i in two]
+    g_relay = copy(G_RELAY, back_out.at[0, part(PIECES - 1)], relay.at[1], z_back)
+    g_passed = copy(G_BACK + PIECES - 1, relay.at[1], back_in.at[0, part(PIECES - 1)], y_back)
     g_far = [copy(G_FAR + i, back_out.at[1, part(i)], back_in.at[1, part(i)], back2_dev) for i in two]
     ig_core = [copy(IG_CORE + i, core_out.at[slot(i)], core_in.at[slot(i)], core_dev) for i in range(4)]
-    ig_back = [copy(IG + i, img_out.at[i], img_in.at[i], img_devs[i]) for i in range(3)]
-
+    ig_a = copy(IG, img_out.at[0], img_in.at[0], a_dev)
+    ig_z = copy(IG + 1, img_out.at[1], img_in.at[1], z_dev)
+    ig_az = copy(IG + 2, img_out.at[2], img_in.at[2], a_dev)
+
+    pl.when(last)(t_relay.start)
+    for i in two[:-1]:
+        t_next[i].start()
+    pl.when(jnp.logical_not(last))(t_next[-1].start)
     for i in two:
-        t_next[i].start()
-    for i in (2, 0, 1):
-        images[i].start()
+        img_z[i].start()
+    img_a.start()
+    for i in range(3):
         params[i].start()
     t_side.start()
     img_core[0].start()
 
     for i in two:
+        if i == PIECES - 1:
+
+            @pl.when(last)
+            def _():
+                t_relay.wait_recv()
+                t_passed.start()
+
+        img_z[i].wait_recv()
+        img_az[i].start()
         t_next[i].wait_recv()
         pl.when(c == 1)(t_far[i].start)
         t_hop[i].start()
-    for i in (0, 1, 2):
-        images[i].wait_recv()
-        img_core[i + 1].start()
+    img_core[2].start()
+    img_a.wait_recv()
+    img_core[1].start()
+    for i in two:
+        img_az[i].wait_recv()
+    img_core[3].start()
+    for i in range(3):
         params[i].wait_recv()
     prm_core.start()
 
@@ -216,15 +268,26 @@
         core_out[slot(i)] = ig[1 - c, slot(i)].astype(BF16)
         ig_core[i].start()
 
-    for i in (3, 1, 2):
+    for i, send in ((3, ig_az), (1, ig_a)):
         ig_core[i].wait_recv()
         img_out[i - 1] = (ig[c, slot(i)] + core_in[slot(i)].astype(F32)).astype(BF16)
-        ig_back[i - 1].start()
+        send.start()
+    ig_core[2].wait_recv()
+    ig[c, slot(2)] += core_in[slot(2)].astype(F32)
 
     for i in two:
         g_hop[i].wait_recv()
         back_out[0, part(i)] = (tg[1, part(i)] + hop_in[0, part(i)].astype(F32)).astype(BF16)
-        g_back[i].start()
+        if i < PIECES - 1:
+            g_back[i].start()
+        else:
+            pl.when(jnp.logical_not(first))(g_back[i].start)
+
+            @pl.when(first)
+            def _():
+                pl.semaphore_wait(ready, 1)
+                g_relay.start()
+
 
     @pl.when(c == 1)
     def _():
@@ -233,16 +296,23 @@
             back_out[1, part(i)] = (tg[2, part(i)] + hop_in[1, part(i)].astype(F32)).astype(BF16)
             g_far[i].start()
 
+    ig_az.wait_recv()
+    img_out[1] = (ig[c, slot(2)] + img_in[2].astype(F32)).astype(BF16)
+    ig_z.start()
+
+    @pl.when(first)
+    def _():
+        g_relay.wait_recv()
+        g_passed.start()
+
     ig_core[0].wait_recv()
     ig[c, own] += core_in[own].astype(F32)
     g_side.wait_recv()
     tg[0, own] += side_in[...].astype(F32)
 
-    for i in range(3):
-        ig_back[i].wait_recv()
-    image_out[...] = (
-        (ig[c, own] + img_in[0].astype(F32)) + (img_in[1].astype(F32) + img_in[2].astype(F32))
-    ).astype(BF16)
+    ig_a.wait_recv()
+    ig_z.wait_recv()
+    image_out[...] = ((ig[c, own] + img_in[0].astype(F32)) + img_in[1].astype(F32)).astype(BF16)
 
     for i in two:
         g_back[i].wait_recv()
@@ -257,9 +327,12 @@
             g_far[i].wait_recv()
         text_out[...] = ((tg[0, own] + back_in[0].astype(F32)) + back_in[1].astype(F32)).astype(BF16)
 
-    for sent in (t_side, *t_next, *t_hop, *images, *params, *img_core, prm_core, g_side, *g_hop, *g_back,
-                 *ig_core, *ig_back):
+    for sent in (t_side, *t_next, *t_hop, img_a, *img_z, *img_az, *params, *img_core, prm_core, g_side, *g_hop, *g_back,
+                 *ig_core, ig_a, ig_z, ig_az):
         sent.wait_send()
+
+    pl.when(last)(t_relay.wait_send)
+    pl.when(first)(g_relay.wait_send)
 
     @pl.when(c == 1)
     def _():
@@ -297,12 +370,14 @@
                 pltpu.VMEM((2, rows, width), BF16),
                 pltpu.VMEM((3, rows, width), BF16),
                 pltpu.VMEM((3, rows, width), BF16),
+                pltpu.VMEM((2, rows // PIECES, width), BF16),
                 pltpu.SemaphoreType.DMA((5,)),
                 pltpu.SemaphoreType.DMA((N_COPIES,)),
                 pltpu.SemaphoreType.DMA((N_COPIES,)),
+                pltpu.SemaphoreType.REGULAR,
             ],
             compiler_params=pltpu.CompilerParams(
-                collective_id=0, has_side_effects=True, vmem_limit_bytes=40 * 2**20
+                collective_id=0, has_side_effects=True, vmem_limit_bytes=60 * 2**20
             ),
             name="window_loss_grad",
         )(

time: 57.7 us -> 53.5 us (0.927)
  the two profiles are of different devices: /device:TPU:1 before, /device:TPU:57 now
where the time goes in v3:
time: 53.5 us; the launch traced here: 53.4 us
  Pallas kernels  49.7 us (93%)
  local copies, waits for them, and re-layouts  2.34 us (4%)
  between operations  1.3 us (2%)
    pallas_call x1, Pallas kernels, per_device(): pl.pallas_call(functools.partial(kernel, n_blk), out_shape=(jax.ShapeDtyp...  49.7 us
    unnamed x4, local copies, waits for them, and re-layouts  2.34 us

profile of v3, /device:TPU:57, one launch (start us, length us, event | category | flops | bytes accessed | tf_op | source)
XLA Modules:
  0.0 53.4 jit_solution(13552759068560532446)
XLA Ops:
  1.3 49.7 %window_loss_grad.1 = (bf16[128,768]{1,0:T(8,128)(2,1)}, bf16[128,768]{1,0:T(8,128)(2,1)}) custom-call(f32[1,1]{1,0:T(1,128)} %bitcast.4.scale_ref, bf16[128,768]{1,0:T(8,128)(2,1)} %image_ref.1, bf16[128,768]{1,0:T(8,128)(2,1)} %text_ref.1, f32[1,128]{1,0:T(1,128)} %bitcast.5, f32[1,128]{1,0:T(1,128)} %bitcast.6, s32[1,128]{1,0:T(1,128)} %bitcast.7), custom_call_target="tpu_custom_call" | custom-call | tf_op jit(solution)/shard_map/window_loss_grad/pallas_call | solution.py:349
  51.0 0.0 copy-start
  51.0 1.7 %copy.11 = bf16[128,768]{1,0:T(8,128)(2,1)} copy(bf16[128,768]{1,0:T(8,128)(2,1)} %get-tuple-element.4) | data formatting | bytes 393216
  52.7 0.0 copy-done
  52.7 0.7 %copy.12 = bf16[128,768]{1,0:T(8,128)(2,1)} copy(bf16[128,768]{1,0:T(8,128)(2,1)S(1)} %copy-done) | data formatting | bytes 393216
Async XLA Ops:
  51.0 1.7 %copy-start = (bf16[128,768]{1,0:T(8,128)(2,1)S(1)}, bf16[128,768]{1,0:T(8,128)(2,1)}, u32[]{:S(2)}) copy-start(bf16[128,768]{1,0:T(8,128)(2,1)} %get-tuple-element.5) | copy-start | bytes 589828

commit v4 on v3

v4 whole, which is shorter than its diff:
```python
import functools

import jax
import jax.numpy as jnp
from jax import lax
from jax.experimental import pallas as pl
from jax.experimental.pallas import tpu as pltpu
from jax.sharding import PartitionSpec as P

MESH = pl.DeviceIdType.MESH
F32 = jnp.float32
BF16 = jnp.bfloat16
PIECES = 4
LATER = PIECES // 2
Y = 8

HALF = PIECES // 2

T_SIDE = 0
T_NEXT = 1
T_HOP = T_NEXT + PIECES
T_FAR = T_HOP + PIECES
T_FAR_HOP = T_FAR + PIECES
IMG = T_FAR_HOP + PIECES
IMG_Z = IMG + PIECES
IMG_AZ = IMG_Z + PIECES
PRM = IMG_AZ + PIECES
IMG_CORE = PRM + 3
PRM_CORE = IMG_CORE + 4
G_SIDE = PRM_CORE + 1
G_HOP = G_SIDE + 1
G_BACK = G_HOP + PIECES
G_FAR_HOP = G_BACK + PIECES
G_FAR = G_FAR_HOP + PIECES
IG_CORE = G_FAR + PIECES
IG_A = IG_CORE + 4
IG_Z = IG_A + PIECES
IG_AZ = IG_Z + PIECES
T_RELAY = IG_AZ + PIECES
G_RELAY = T_RELAY + LATER
T_FAR_Z = G_RELAY + LATER
T_FAR_PASSED = T_FAR_Z + PIECES
G_FAR_Z = T_FAR_PASSED + PIECES
N_COPIES = G_FAR_Z + PIECES


def kernel(n_blk, scale_ref, image_ref, text_ref, log_ref, grad_ref, pos_ref, image_out, text_out,
           img, prm, tx, rowv, posv, tg, ig, core_out, core_in, side_out, side_in, hop_out, hop_in,
           back_out, back_in, img_out, img_in, relay, image_vm, text_vm, load_sem, send_sem, recv_sem, ready):
    rows = image_ref.shape[0]
    piece = rows // PIECES
    blk, grp = lax.axis_index("blk"), lax.axis_index("group")
    c = blk % 2
    pair = blk // 2
    n_pair = n_blk // 2
    z, x = grp // 4, grp % 4
    x_a = x + 1 - 2 * (x % 2)
    x_b = 3 - x

    def at_pair(step):
        return (((pair + step + n_pair) % n_pair) * 2 + c, grp)

    core_dev = (pair * 2 + 1 - c, grp)
    side_dev = (blk, z * 4 + x_b)
    a_dev, z_dev = (blk, z * 4 + x_a), (blk, (1 - z) * 4 + x)
    img_devs = (a_dev, z_dev, (blk, (1 - z) * 4 + x_a))
    next_dev, back_dev = at_pair(1), at_pair(-1)
    back2_dev = at_pair(-2)
    y = pair % Y
    last, first, before, second = y == Y - 1, y == 0, y == Y - 2, y == 1
    crowded = first | last
    lowest = pair < Y
    z_next, z_back = at_pair(Y), at_pair(-Y)
    y_next, y_back = at_pair((y + 1) % Y - y), at_pair((y + Y - 1) % Y - y)
    y_next2, y_back2 = at_pair((y + 2) % Y - y), at_pair((y + Y - 2) % Y - y)

    own, side = pl.ds(0, rows), pl.ds(rows, rows)

    def slot(i):
        return pl.ds(i * rows, rows)

    def part(i):
        return pl.ds(i * piece, piece)

    def slot_part(s, i):
        return pl.ds(s * rows + i * piece, piece)

    def side_part(i):
        return slot_part(1, i)

    def copy(index, src, dst, device):
        return pltpu.make_async_remote_copy(
            src_ref=src, dst_ref=dst, send_sem=send_sem.at[index], recv_sem=recv_sem.at[index],
            device_id=device, device_id_type=MESH,
        )

    loads = [
        pltpu.make_async_copy(text_ref, tx.at[0, own], load_sem.at[0]),
        pltpu.make_async_copy(image_ref, img.at[c, own], load_sem.at[1]),
        pltpu.make_async_copy(log_ref, rowv.at[0], load_sem.at[2]),
        pltpu.make_async_copy(grad_ref, rowv.at[1], load_sem.at[3]),
        pltpu.make_async_copy(pos_ref, posv, load_sem.at[4]),
    ]
    for load in loads:
        load.start()

    barrier = pltpu.get_barrier_semaphore()
    senders = (core_dev, side_dev, *img_devs, back_dev)
    for device in senders:
        pl.semaphore_signal(barrier, inc=1, device_id=device, device_id_type=MESH)

    @pl.when(last | before | first | second)
    def _():
        pl.semaphore_signal(barrier, inc=1, device_id=z_back, device_id_type=MESH)

    @pl.when(first)
    def _():
        pl.semaphore_signal(barrier, inc=1, device_id=y_back, device_id_type=MESH)
        pl.semaphore_signal(barrier, inc=1, device_id=y_back2, device_id_type=MESH)

    for load in loads:
        load.wait()
    prm[c, 0:1, 0:rows] = rowv[0]
    prm[c, 1:2, 0:rows] = rowv[1]
    prm[c, 2:3, 0:rows] = posv[...].astype(F32)
    prm[c, 3:8, 0:rows] = jnp.zeros((5, rows), F32)
    pl.semaphore_wait(barrier, len(senders) + jnp.where(last | before, 2, jnp.where(first | second, 1, 0)))

    @pl.when(first | (second & (c == 1)))
    def _():
        pl.semaphore_signal(ready, inc=1, device_id=z_next, device_id_type=MESH)

    scale = scale_ref[0, 0]
    base_own = (grp * rows).astype(F32)
    base_side = ((z * 4 + x_b) * rows).astype(F32)
    two = range(PIECES)

    t_side = copy(T_SIDE, tx.at[0, own], tx.at[0, side], side_dev)
    t_next = [copy(T_NEXT + i, tx.at[0, part(i)], tx.at[1, part(i)], next_dev) for i in two]
    later = range(PIECES - LATER, PIECES)
    t_relay = {i: copy(T_RELAY + i - later[0], tx.at[0, part(i)], relay.at[0, part(i)], z_next) for i in later}
    t_passed = {i: copy(T_NEXT + i, relay.at[0, part(i)], tx.at[1, part(i)], y_next) for i in later}
    t_far_z = [copy(T_FAR_Z + i, tx.at[0, part(i)], relay.at[0, part(i)], z_next) for i in two]
    t_far_passed = [copy(T_FAR_PASSED + i, relay.at[0, part(i)], tx.at[2, part(i)], y_next2) for i in two]
    t_hop = [copy(T_HOP + i, tx.at[1, part(i)], tx.at[1, side_part(i)], side_dev) for i in two]
    t_far = [copy(T_FAR + i, tx.at[1, part(i)], tx.at[2, part(i)], next_dev) for i in two]
    t_far_hop = [copy(T_FAR_HOP + i, tx.at[2, part(i)], tx.at[2, side_part(i)], side_dev) for i in two]
    img_a = [copy(IMG + i, img.at[c, part(i)], img.at[c, slot_part(1, i)], a_dev) for i in two]
    img_z = [copy(IMG_Z + i, img.at[c, part(i)], img.at[c, slot_part(2, i)], z_dev) for i in two]
    img_az = [
        copy(IMG_AZ + i, img.at[c, slot_part(2, i)], img.at[c, slot_part(3, i)], a_dev) for i in two
    ]
    img_za = [copy(IMG_AZ + i, img.at[c, slot_part(1, i)], img.at[c, slot_part(3, i)], z_dev) for i in two]
    params = [copy(PRM + i, prm.at[c, :, own], prm.at[c, :, slot(i + 1)], img_devs[i]) for i in range(3)]
    img_core = [copy(IMG_CORE + i, img.at[c, slot(i)], img.at[c, slot(i)], core_dev) for i in range(4)]
    prm_core = copy(PRM_CORE, prm.at[c], prm.at[c], core_dev)
    img_got = [copy(IMG_CORE + i, img.at[1 - c, slot(i)], img.at[1 - c, slot(i)], core_dev) for i in range(4)]
    prm_got = copy(PRM_CORE, prm.at[1 - c], prm.at[1 - c], core_dev)

    g_side = copy(G_SIDE, side_out, side_in, side_dev)
    g_hop = [copy(G_HOP + i, hop_out.at[0, part(i)], hop_in.at[0, part(i)], side_dev) for i in two]
    g_far_hop = [copy(G_FAR_HOP + i, hop_out.at[1, part(i)], hop_in.at[1, part(i)], side_dev) for i in two]
    g_back = [copy(G_BACK + i, back_out.at[0, part(i)], back_in.at[0, part(i)], back_dev) for i in two]
    g_relay = {i: copy(G_RELAY + i - later[0], back_out.at[0, part(i)], relay.at[1, part(i)], z_back) for i in later}
    g_passed = {i: copy(G_BACK + i, relay.at[1, part(i)], back_in.at[0, part(i)], y_back) for i in later}
    g_far_z = [copy(G_FAR_Z + i, back_out.at[1, part(i)], relay.at[1, part(i)], z_back) for i in two]
    g_far_passed = [copy(G_FAR + i, relay.at[1, part(i)], back_in.at[1, part(i)], y_back2) for i in two]
    g_far = [copy(G_FAR + i, back_out.at[1, part(i)], back_in.at[1, part(i)], back2_dev) for i in two]
    ig_core = [copy(IG_CORE + i, core_out.at[slot(i)], core_in.at[slot(i)], core_dev) for i in range(4)]
    ig_a = [copy(IG_A + i, img_out.at[0, part(i)], img_in.at[0, part(i)], a_dev) for i in two]
    ig_z = [copy(IG_Z + i, img_out.at[1, part(i)], img_in.at[1, part(i)], z_dev) for i in two]
    ig_az = [
        copy(IG_AZ + i, img_out.at[2, part(i)], img_in.at[2, part(i)], a_dev) for i in two
    ]
    ig_za = [copy(IG_AZ + i, img_out.at[2, part(i)], img_in.at[2, part(i)], z_dev) for i in two]
    free = jnp.logical_not(crowded)

    for i in later:
        pl.when(last)(t_relay[i].start)
    for i in two:
        if i in later:
            pl.when(jnp.logical_not(last))(t_next[i].start)
        else:
            t_next[i].start()
    for i in two:
        pl.when(before & (c == 1))(t_far_z[i].start)
    early, late = two[:HALF], two[HALF:]
    for i, k in zip(early, late):
        img_z[i].start()
        img_a[k].start()
    for i, k in zip(early, late):
        img_z[k].start()
        img_a[i].start()
    for i in range(3):
        params[i].start()
    t_side.start()
    img_core[0].start()
    tg[...] = jnp.zeros_like(tg)
    ig[...] = jnp.zeros_like(ig)

    def pass_relayed():
        for i in later:
            t_relay[i].wait_recv()
            t_passed[i].start()

    def pass_far_relayed():
        for i in two:
            t_far_z[i].wait_recv()
            t_far_passed[i].start()

    def pass_next():
        for i in two:
            if i == later[0]:
                pl.when(last & jnp.logical_not(lowest))(pass_relayed)
            t_next[i].wait_recv()
            pl.when((c == 1) & jnp.logical_not(last))(t_far[i].start)
            t_hop[i].start()
        pl.when(before & jnp.logical_not(lowest) & (c == 1))(pass_far_relayed)

    def pass_far():
        for i in two:
            pl.when(first)(t_far_passed[i].wait_recv)
            pl.when(jnp.logical_not(first))(t_far[i].wait_recv)
            t_far_hop[i].start()

    for i, k in zip(early, late):
        img_z[i].wait_recv()
        img_az[i].start()
        @pl.when(free)
        def _():
            img_a[k].wait_recv()
            img_za[k].start()

        @pl.when(crowded)
        def _():
            img_z[k].wait_recv()
            img_az[k].start()

    pl.when(jnp.logical_not(first))(pass_next)
    for i in early:
        img_a[i].wait_recv()
    pl.when(free)(img_core[1].start)
    for i in late:
        pl.when(crowded)(img_a[i].wait_recv)
    pl.when(crowded)(img_core[1].start)
    for i in late:
        pl.when(free)(img_z[i].wait_recv)
    img_core[2].start()
    for i in two:
        img_az[i].wait_recv()
    img_core[3].start()
    for i in range(3):
        params[i].wait_recv()
    prm_core.start()
    pl.when(first)(pass_next)
    pl.when(first & (c == 1))(pass_far)
    pl.when(last & lowest)(pass_relayed)
    pl.when(before & lowest & (c == 1))(pass_far_relayed)
    t_side.wait_recv()

    def tile(s, _):
        j = (s + 1) // 2 - (s // 3) * (2 - 2 * c)
        other = s // 2
        i = c + other * (1 - 2 * c)

        @pl.when(s == 1)
        def _():
            pl.when((c == 1) & jnp.logical_not(first | second))(pass_far)
            for q in two:
                t_hop[q].wait_recv()

        @pl.when(s == 2)
        def _():
            for q in range(4):
                img_got[q].wait_recv()
            prm_got.wait_recv()

        @pl.when((s == 3) & (c == 1))
        def _():
            pl.when(second)(pass_far)
            for q in two:
                t_far_hop[q].wait_recv()

        scores = lax.dot_general(tx[j], img[i], (((1,), (1,)), ((), ())), preferred_element_type=F32)
        prob = jnp.exp(scale * scores - prm[i, 0:1, :])
        row = lax.broadcasted_iota(jnp.int32, scores.shape, 0)
        place = jnp.where(row < rows, row.astype(F32) + base_own, (row - rows).astype(F32) + base_side)
        place = place + (s * 65536).astype(F32)
        prob = prob - jnp.where(place == prm[i, 2:3, :], 1.0, 0.0)
        weight = (prob * (scale * prm[i, 1:2, :])).astype(BF16)
        tg[j] += jnp.dot(weight, img[i], preferred_element_type=F32)
        ig[i] += lax.dot_general(weight, tx[j], (((0,), (0,)), ((), ())), preferred_element_type=F32)

        @pl.when((s == 0) & (c == 1))
        def _():
            side_out[...] = tg[0, side].astype(BF16)
            g_side.start()

        @pl.when(s == 2)
        def _():
            for q in two:
                hop_out[0, part(q)] = tg[1, side_part(q)].astype(BF16)
                g_hop[q].start()

        @pl.when((s == 3) & (c == 1))
        def _():
            for q in two:
                hop_out[1, part(q)] = tg[2, side_part(q)].astype(BF16)
                g_far_hop[q].start()

        return 0

    lax.fori_loop(0, 4, tile, 0)

    for i in (3, 1, 2, 0):
        core_out[slot(i)] = ig[1 - c, slot(i)].astype(BF16)
        ig_core[i].start()

    def ready_part(n, i):
        return ig[c, slot_part(n, i)] + core_in[slot_part(n, i)].astype(F32)

    ig_core[3].wait_recv()
    for i, k in zip(early, late):
        for q in (i, k):
            img_out[2, part(q)] = ready_part(3, q).astype(BF16)
        ig_az[i].start()
        pl.when(crowded)(ig_az[k].start)
        pl.when(free)(ig_za[k].start)
    ig_core[1].wait_recv()
    ig_core[2].wait_recv()
    for i, k in zip(early, late):
        img_out[0, part(i)] = ready_part(1, i).astype(BF16)
        ig_a[i].start()

        @pl.when(free)
        def _():
            img_out[1, part(k)] = ready_part(2, k).astype(BF16)
            ig_z[k].start()

        @pl.when(crowded)
        def _():
            img_out[0, part(k)] = ready_part(1, k).astype(BF16)
            ig_a[k].start()

    for i in two:
        g_hop[i].wait_recv()
        back_out[0, part(i)] = (tg[1, part(i)] + hop_in[0, part(i)].astype(F32)).astype(BF16)
        if i in later:
            pl.when(jnp.logical_not(first))(g_back[i].start)

            @pl.when(first)
            def _():
                if i == later[0]:
                    pl.semaphore_wait(ready, 1)
                g_relay[i].start()
        else:
            g_back[i].start()

    @pl.when(c == 0)
    def _():
        side_out[...] = tg[0, side].astype(BF16)
        g_side.start()

    def far_back(i):
        @pl.when(c == 1)
        def _():
            g_far_hop[i].wait_recv()
            back_out[1, part(i)] = (tg[2, part(i)] + hop_in[1, part(i)].astype(F32)).astype(BF16)
            pl.when(jnp.logical_not(second))(g_far[i].start)

            @pl.when(second)
            def _():
                if i == 0:
                    pl.semaphore_wait(ready, 1)
                g_far_z[i].start()

    for i, k in zip(early, late):
        far_back(2 * i)
        ig_az[i].wait_recv()
        img_out[1, part(i)] = (ready_part(2, i) + img_in[2, part(i)].astype(F32)).astype(BF16)
        ig_z[i].start()
        far_back(2 * i + 1)
        ig_az[k].wait_recv()

        @pl.when(free)
        def _():
            img_out[0, part(k)] = (ready_part(1, k) + img_in[2, part(k)].astype(F32)).astype(BF16)
            ig_a[k].start()

        @pl.when(crowded)
        def _():
            img_out[1, part(k)] = (ready_part(2, k) + img_in[2, part(k)].astype(F32)).astype(BF16)
            ig_z[k].start()

    @pl.when(first)
    def _():
        for i in later:
            g_relay[i].wait_recv()
            g_passed[i].start()

    @pl.when(second & (c == 1))
    def _():
        for i in two:
            g_far_z[i].wait_recv()
            g_far_passed[i].start()

    ig_core[0].wait_recv()
    ig[c, own] += core_in[own].astype(F32)
    g_side.wait_recv()
    tg[0, own] += side_in[...].astype(F32)

    for i in two:
        ig_a[i].wait_recv()
        ig_z[i].wait_recv()
    image_vm[...] = ((ig[c, own] + img_in[0].astype(F32)) + img_in[1].astype(F32)).astype(BF16)

    image_store = pltpu.make_async_copy(image_vm, image_out, load_sem.at[0])
    image_store.start()
    for i in two:
        g_back[i].wait_recv()

    @pl.when(c == 0)
    def _():
        text_vm[...] = (tg[0, own] + back_in[0].astype(F32)).astype(BF16)

    @pl.when(c == 1)
    def _():
        for i in two:
            g_far[i].wait_recv()
        text_vm[...] = ((tg[0, own] + back_in[0].astype(F32)) + back_in[1].astype(F32)).astype(BF16)

    text_store = pltpu.make_async_copy(text_vm, text_out, load_sem.at[1])
    text_store.start()

    for sent in (t_side, *t_next, *t_hop, *img_a, *img_z, *img_az, *params, *img_core, prm_core, g_side, *g_hop, *g_back,
                 *ig_core, *ig_a, *ig_z, *ig_az):
        sent.wait_send()

    for i in later:
        pl.when(last)(t_relay[i].wait_send)
        pl.when(first)(g_relay[i].wait_send)

    @pl.when(c == 1)
    def _():
        for sent in (*t_far_hop, *g_far_hop, *g_far):
            sent.wait_send()
        for sent in g_far_z:
            pl.when(second)(sent.wait_send)
        for i in two:
            pl.when(jnp.logical_not(last))(t_far[i].wait_send)
            pl.when(before)(t_far_z[i].wait_send)
            pl.when(before)(t_far_passed[i].wait_send)
    image_store.wait()
    text_store.wait()


def hand_over(image_ref, text_ref, image_out, text_out, held, load_sem, store_sem):
    half = image_ref.shape[0] // 2
    pieces = [(n, i) for n in range(2) for i in range(2)]
    loads, stores = [], []
    for n, i in pieces:
        rows = pl.ds(i * half, half)
        source, target = (image_ref, image_out) if n == 0 else (text_ref, text_out)
        k = 2 * n + i
        loads.append(pltpu.make_async_copy(source.at[rows], held.at[k], load_sem.at[k]))
        stores.append(pltpu.make_async_copy(held.at[k], target.at[rows], store_sem.at[k]))
    for load in loads:
        load.start()
    for load, store in zip(loads, stores):
        load.wait()
        store.start()
    for store in stores:
        store.wait()


def solution(mesh):
    n_blk = mesh.shape["blk"]

    def per_device(image_rows, text_rows, log_norm, row_grad, pos_index, logit_scale):
        rows, width = image_rows.shape
        anywhere = pl.BlockSpec(memory_space=pltpu.HBM)
        grads = pl.pallas_call(
            functools.partial(kernel, n_blk),
            out_shape=(jax.ShapeDtypeStruct((rows, width), BF16),) * 2,
            in_specs=[pl.BlockSpec(memory_space=pltpu.SMEM)] + [anywhere] * 5,
            out_specs=(anywhere,) * 2,
            scratch_shapes=[
                pltpu.VMEM((2, 4 * rows, width), BF16),
                pltpu.VMEM((2, 8, 4 * rows), F32),
                pltpu.VMEM((3, 2 * rows, width), BF16),
                pltpu.VMEM((2, 1, rows), F32),
                pltpu.VMEM((1, rows), jnp.int32),
                pltpu.VMEM((3, 2 * rows, width), F32),
                pltpu.VMEM((2, 4 * rows, width), F32),
                pltpu.VMEM((4 * rows, width), BF16),
                pltpu.VMEM((4 * rows, width), BF16),
                pltpu.VMEM((rows, width), BF16),
                pltpu.VMEM((rows, width), BF16),
                pltpu.VMEM((2, rows, width), BF16),
                pltpu.VMEM((2, rows, width), BF16),
                pltpu.VMEM((2, rows, width), BF16),
                pltpu.VMEM((2, rows, width), BF16),
                pltpu.VMEM((3, rows, width), BF16),
                pltpu.VMEM((3, rows, width), BF16),
                pltpu.VMEM((2, rows, width), BF16),
                pltpu.VMEM((rows, width), BF16),
                pltpu.VMEM((rows, width), BF16),
                pltpu.SemaphoreType.DMA((5,)),
                pltpu.SemaphoreType.DMA((N_COPIES,)),
                pltpu.SemaphoreType.DMA((N_COPIES,)),
                pltpu.SemaphoreType.REGULAR,
            ],
            compiler_params=pltpu.CompilerParams(
                collective_id=0, has_side_effects=True, vmem_limit_bytes=60 * 2**20
            ),
            name="window_loss_grad",
        )(
            logit_scale.reshape(1, 1), image_rows, text_rows, log_norm.reshape(1, rows),
            row_grad.reshape(1, rows), pos_index.reshape(1, rows),
        )
        return pl.pallas_call(
            hand_over,
            out_shape=(jax.ShapeDtypeStruct((rows, width), BF16),) * 2,
            in_specs=[anywhere] * 2,
            out_specs=(anywhere,) * 2,
            scratch_shapes=[
                pltpu.VMEM((4, rows // 2, width), BF16),
                pltpu.SemaphoreType.DMA((4,)),
                pltpu.SemaphoreType.DMA((4,)),
            ],
            compiler_params=pltpu.CompilerParams(vmem_limit_bytes=60 * 2**20),
            name="hand_over",
        )(*grads)

    return jax.shard_map(
        per_device,
        mesh=mesh,
        in_specs=(
            P(("blk", "group"), None),
            P(("blk", "group"), None),
            P(("blk", "group")),
            P(("blk", "group")),
            P(("blk", "group")),
            P(),
        ),
        out_specs=(P(("blk", "group"), None), P(("blk", "group"), None)),
        check_vma=False,
    )
```

time: 53.5 us -> 51.4 us (0.961)
  the two profiles are of different devices: /device:TPU:57 before, /device:TPU:1 now
where the time goes in v4:
time: 51.4 us; the launch traced here: 51.2 us
  Pallas kernels  50 us (97%)
  between operations  1.29 us (3%)
    pallas_call x1, Pallas kernels, per_device(): pl.pallas_call(functools.partial(kernel, n_blk), out_shape=(jax.ShapeDtyp...  48.2 us
    pallas_call x1, Pallas kernels, per_device(): pl.pallas_call(hand_over, out_shape=(jax.ShapeDtypeStruct((rows, width),...  1.75 us

profile of v4, /device:TPU:1, one launch (start us, length us, event | category | flops | bytes accessed | tf_op | source)
XLA Modules:
  0.0 51.2 jit_solution(12510479345710697904)
XLA Ops:
  1.3 48.2 %window_loss_grad.1 = (bf16[128,768]{1,0:T(8,128)(2,1)}, bf16[128,768]{1,0:T(8,128)(2,1)}) custom-call(f32[1,1]{1,0:T(1,128)} %bitcast.4.scale_ref, bf16[128,768]{1,0:T(8,128)(2,1)} %image_ref.1, bf16[128,768]{1,0:T(8,128)(2,1)} %text_ref.1, f32[1,128]{1,0:T(1,128)} %bitcast.5, f32[1,128]{1,0:T(1,128)} %bitcast.6, s32[1,128]{1,0:T(1,128)} %bitcast.7), custom_call_target="tpu_custom_call" | custom-call | tf_op jit(solution)/shard_map/window_loss_grad/pallas_call | solution.py:482
  49.5 1.7 %hand_over.1 = (bf16[128,768]{1,0:T(8,128)(2,1)}, bf16[128,768]{1,0:T(8,128)(2,1)}) custom-call(bf16[128,768]{1,0:T(8,128)(2,1)} %get-tuple-element.4.image_ref, bf16[128,768]{1,0:T(8,128)(2,1)} %get-tuple-element.5.text_ref), custom_call_target="tpu_custom_call" | custom-call | tf_op jit(solution)/shard_map/hand_over/pallas_call | solution.py:521

commit v5 on v4

--- a/solution.py
+++ b/solution.py
@@ -11,7 +11,8 @@
 F32 = jnp.float32
 BF16 = jnp.bfloat16
 PIECES = 4
-LATER = PIECES // 2
+LATER = 2
+BACK_LATER = 1
 Y = 8
 
 HALF = PIECES // 2
@@ -38,7 +39,7 @@
 IG_AZ = IG_Z + PIECES
 T_RELAY = IG_AZ + PIECES
 G_RELAY = T_RELAY + LATER
-T_FAR_Z = G_RELAY + LATER
+T_FAR_Z = G_RELAY + BACK_LATER
 T_FAR_PASSED = T_FAR_Z + PIECES
 G_FAR_Z = T_FAR_PASSED + PIECES
 N_COPIES = G_FAR_Z + PIECES
@@ -101,9 +102,6 @@
         pltpu.make_async_copy(grad_ref, rowv.at[1], load_sem.at[3]),
         pltpu.make_async_copy(pos_ref, posv, load_sem.at[4]),
     ]
-    for load in loads:
-        load.start()
-
     barrier = pltpu.get_barrier_semaphore()
     senders = (core_dev, side_dev, *img_devs, back_dev)
     for device in senders:
@@ -118,6 +116,8 @@
         pl.semaphore_signal(barrier, inc=1, device_id=y_back, device_id_type=MESH)
         pl.semaphore_signal(barrier, inc=1, device_id=y_back2, device_id_type=MESH)
 
+    for load in loads:
+        load.start()
     for load in loads:
         load.wait()
     prm[c, 0:1, 0:rows] = rowv[0]
@@ -138,6 +138,8 @@
     t_side = copy(T_SIDE, tx.at[0, own], tx.at[0, side], side_dev)
     t_next = [copy(T_NEXT + i, tx.at[0, part(i)], tx.at[1, part(i)], next_dev) for i in two]
     later = range(PIECES - LATER, PIECES)
+    by_z = {i: last & ((z == 1) | (i == later[-1])) for i in later}
+    back_later = range(PIECES - BACK_LATER, PIECES)
     t_relay = {i: copy(T_RELAY + i - later[0], tx.at[0, part(i)], relay.at[0, part(i)], z_next) for i in later}
     t_passed = {i: copy(T_NEXT + i, relay.at[0, part(i)], tx.at[1, part(i)], y_next) for i in later}
     t_far_z = [copy(T_FAR_Z + i, tx.at[0, part(i)], relay.at[0, part(i)], z_next) for i in two]
@@ -161,8 +163,8 @@
     g_hop = [copy(G_HOP + i, hop_out.at[0, part(i)], hop_in.at[0, part(i)], side_dev) for i in two]
     g_far_hop = [copy(G_FAR_HOP + i, hop_out.at[1, part(i)], hop_in.at[1, part(i)], side_dev) for i in two]
     g_back = [copy(G_BACK + i, back_out.at[0, part(i)], back_in.at[0, part(i)], back_dev) for i in two]
-    g_relay = {i: copy(G_RELAY + i - later[0], back_out.at[0, part(i)], relay.at[1, part(i)], z_back) for i in later}
-    g_passed = {i: copy(G_BACK + i, relay.at[1, part(i)], back_in.at[0, part(i)], y_back) for i in later}
+    g_relay = {i: copy(G_RELAY + i - back_later[0], back_out.at[0, part(i)], relay.at[1, part(i)], z_back) for i in back_later}
+    g_passed = {i: copy(G_BACK + i, relay.at[1, part(i)], back_in.at[0, part(i)], y_back) for i in back_later}
     g_far_z = [copy(G_FAR_Z + i, back_out.at[1, part(i)], relay.at[1, part(i)], z_back) for i in two]
     g_far_passed = [copy(G_FAR + i, relay.at[1, part(i)], back_in.at[1, part(i)], y_back2) for i in two]
     g_far = [copy(G_FAR + i, back_out.at[1, part(i)], back_in.at[1, part(i)], back2_dev) for i in two]
@@ -176,10 +178,10 @@
     free = jnp.logical_not(crowded)
 
     for i in later:
-        pl.when(last)(t_relay[i].start)
+        pl.when(by_z[i])(t_relay[i].start)
     for i in two:
         if i in later:
-            pl.when(jnp.logical_not(last))(t_next[i].start)
+            pl.when(jnp.logical_not(by_z[i]))(t_next[i].start)
         else:
             t_next[i].start()
     for i in two:
@@ -200,8 +202,12 @@
 
     def pass_relayed():
         for i in later:
-            t_relay[i].wait_recv()
-            t_passed[i].start()
+
+            @pl.when(by_z[i])
+            def _():
+                t_relay[i].wait_recv()
+                t_passed[i].start()
+
 
     def pass_far_relayed():
         for i in two:
@@ -253,7 +259,6 @@
         params[i].wait_recv()
     prm_core.start()
     pl.when(first)(pass_next)
-    pl.when(first & (c == 1))(pass_far)
     pl.when(last & lowest)(pass_relayed)
     pl.when(before & lowest & (c == 1))(pass_far_relayed)
     t_side.wait_recv()
@@ -274,6 +279,10 @@
             for q in range(4):
                 img_got[q].wait_recv()
             prm_got.wait_recv()
+
+        @pl.when((s == 2) & (c == 1) & first)
+        def _():
+            pass_far()
 
         @pl.when((s == 3) & (c == 1))
         def _():
@@ -345,12 +354,12 @@
     for i in two:
         g_hop[i].wait_recv()
         back_out[0, part(i)] = (tg[1, part(i)] + hop_in[0, part(i)].astype(F32)).astype(BF16)
-        if i in later:
+        if i in back_later:
             pl.when(jnp.logical_not(first))(g_back[i].start)
 
             @pl.when(first)
             def _():
-                if i == later[0]:
+                if i == back_later[0]:
                     pl.semaphore_wait(ready, 1)
                 g_relay[i].start()
         else:
@@ -392,9 +401,23 @@
             img_out[1, part(k)] = (ready_part(2, k) + img_in[2, part(k)].astype(F32)).astype(BF16)
             ig_z[k].start()
 
+    for sent in (t_side, *t_next, *t_hop, *img_a, *img_z, *img_az, *params, *img_core, prm_core, g_side, *g_hop, *ig_core):
+        sent.wait_send()
+    for i in later:
+        pl.when(by_z[i])(t_relay[i].wait_send)
+
+    @pl.when(c == 1)
+    def _():
+        for sent in (*t_far_hop, *g_far_hop):
+            sent.wait_send()
+        for i in two:
+            pl.when(jnp.logical_not(last))(t_far[i].wait_send)
+            pl.when(before)(t_far_z[i].wait_send)
+            pl.when(before)(t_far_passed[i].wait_send)
+
     @pl.when(first)
     def _():
-        for i in later:
+        for i in back_later:
             g_relay[i].wait_recv()
             g_passed[i].start()
 
@@ -416,6 +439,18 @@
 
     image_store = pltpu.make_async_copy(image_vm, image_out, load_sem.at[0])
     image_store.start()
+    for sent in (*g_back, *ig_a, *ig_z, *ig_az):
+        sent.wait_send()
+    for i in back_later:
+        pl.when(first)(g_relay[i].wait_send)
+
+    @pl.when(c == 1)
+    def _():
+        for sent in g_far:
+            sent.wait_send()
+        for sent in g_far_z:
+            pl.when(second)(sent.wait_send)
+
     for i in two:
         g_back[i].wait_recv()
 
@@ -432,24 +467,6 @@
     text_store = pltpu.make_async_copy(text_vm, text_out, load_sem.at[1])
     text_store.start()
 
-    for sent in (t_side, *t_next, *t_hop, *img_a, *img_z, *img_az, *params, *img_core, prm_core, g_side, *g_hop, *g_back,
-                 *ig_core, *ig_a, *ig_z, *ig_az):
-        sent.wait_send()
-
-    for i in later:
-        pl.when(last)(t_relay[i].wait_send)
-        pl.when(first)(g_relay[i].wait_send)
-
-    @pl.when(c == 1)
-    def _():
-        for sent in (*t_far_hop, *g_far_hop, *g_far):
-            sent.wait_send()
-        for sent in g_far_z:
-            pl.when(second)(sent.wait_send)
-        for i in two:
-            pl.when(jnp.logical_not(last))(t_far[i].wait_send)
-            pl.when(before)(t_far_z[i].wait_send)
-            pl.when(before)(t_far_passed[i].wait_send)
     image_store.wait()
     text_store.wait()
 

time: 51.4 us -> 50.1 us (0.975)
  Pallas kernels: 50 us -> 48.5 us
    pallas_call x1, Pallas kernels: 48.2 us -> 46.7 us  [per_device(): pl.pallas_call(functools.partial(kernel, n_blk), out_shape=(jax.ShapeDtyp...]
where the time goes in v5:
time: 50.1 us; the launch traced here: 49.8 us
  Pallas kernels  48.5 us (97%)
  between operations  1.29 us (3%)
    pallas_call x1, Pallas kernels, per_device(): pl.pallas_call(functools.partial(kernel, n_blk), out_shape=(jax.ShapeDtyp...  46.7 us
    pallas_call x1, Pallas kernels, per_device(): pl.pallas_call(hand_over, out_shape=(jax.ShapeDtypeStruct((rows, width),...  1.75 us

profile of v5, /device:TPU:1, one launch (start us, length us, event | category | flops | bytes accessed | tf_op | source)
XLA Modules:
  0.0 49.8 jit_solution(1517571395969408283)
XLA Ops:
  1.3 46.7 %window_loss_grad.1 = (bf16[128,768]{1,0:T(8,128)(2,1)}, bf16[128,768]{1,0:T(8,128)(2,1)}) custom-call(f32[1,1]{1,0:T(1,128)} %bitcast.4.scale_ref, bf16[128,768]{1,0:T(8,128)(2,1)} %image_ref.1, bf16[128,768]{1,0:T(8,128)(2,1)} %text_ref.1, f32[1,128]{1,0:T(1,128)} %bitcast.5, f32[1,128]{1,0:T(1,128)} %bitcast.6, s32[1,128]{1,0:T(1,128)} %bitcast.7), custom_call_target="tpu_custom_call" | custom-call | tf_op jit(solution)/shard_map/window_loss_grad/pallas_call | solution.py:499
  48.0 1.7 %hand_over.1 = (bf16[128,768]{1,0:T(8,128)(2,1)}, bf16[128,768]{1,0:T(8,128)(2,1)}) custom-call(bf16[128,768]{1,0:T(8,128)(2,1)} %get-tuple-element.4.image_ref, bf16[128,768]{1,0:T(8,128)(2,1)} %get-tuple-element.5.text_ref), custom_call_target="tpu_custom_call" | custom-call | tf_op jit(solution)/shard_map/hand_over/pallas_call | solution.py:538

commit v6 on v5

--- a/solution.py
+++ b/solution.py
@@ -42,7 +42,9 @@
 T_FAR_Z = G_RELAY + BACK_LATER
 T_FAR_PASSED = T_FAR_Z + PIECES
 G_FAR_Z = T_FAR_PASSED + PIECES
-N_COPIES = G_FAR_Z + PIECES
+T_DIRECT = G_FAR_Z + PIECES
+T_PASSED = T_DIRECT + PIECES
+N_COPIES = T_PASSED
 
 
 def kernel(n_blk, scale_ref, image_ref, text_ref, log_ref, grad_ref, pos_ref, image_out, text_out,
@@ -66,10 +68,10 @@
     a_dev, z_dev = (blk, z * 4 + x_a), (blk, (1 - z) * 4 + x)
     img_devs = (a_dev, z_dev, (blk, (1 - z) * 4 + x_a))
     next_dev, back_dev = at_pair(1), at_pair(-1)
-    back2_dev = at_pair(-2)
+    next2_dev, back2_dev = at_pair(2), at_pair(-2)
     y = pair % Y
     last, first, before, second = y == Y - 1, y == 0, y == Y - 2, y == 1
-    crowded = first | last
+    crowded = first
     lowest = pair < Y
     z_next, z_back = at_pair(Y), at_pair(-Y)
     y_next, y_back = at_pair((y + 1) % Y - y), at_pair((y + Y - 1) % Y - y)
@@ -116,6 +118,10 @@
         pl.semaphore_signal(barrier, inc=1, device_id=y_back, device_id_type=MESH)
         pl.semaphore_signal(barrier, inc=1, device_id=y_back2, device_id_type=MESH)
 
+    @pl.when(second)
+    def _():
+        pl.semaphore_signal(barrier, inc=1, device_id=back2_dev, device_id_type=MESH)
+
     for load in loads:
         load.start()
     for load in loads:
@@ -124,7 +130,7 @@
     prm[c, 1:2, 0:rows] = rowv[1]
     prm[c, 2:3, 0:rows] = posv[...].astype(F32)
     prm[c, 3:8, 0:rows] = jnp.zeros((5, rows), F32)
-    pl.semaphore_wait(barrier, len(senders) + jnp.where(last | before, 2, jnp.where(first | second, 1, 0)))
+    pl.semaphore_wait(barrier, len(senders) + jnp.where(last, 3, jnp.where(before, 2, jnp.where(first | second, 1, 0))))
 
     @pl.when(first | (second & (c == 1)))
     def _():
@@ -139,11 +145,12 @@
     t_next = [copy(T_NEXT + i, tx.at[0, part(i)], tx.at[1, part(i)], next_dev) for i in two]
     later = range(PIECES - LATER, PIECES)
     by_z = {i: last & ((z == 1) | (i == later[-1])) for i in later}
-    back_later = range(PIECES - BACK_LATER, PIECES)
+    back_later = range(BACK_LATER)
     t_relay = {i: copy(T_RELAY + i - later[0], tx.at[0, part(i)], relay.at[0, part(i)], z_next) for i in later}
     t_passed = {i: copy(T_NEXT + i, relay.at[0, part(i)], tx.at[1, part(i)], y_next) for i in later}
     t_far_z = [copy(T_FAR_Z + i, tx.at[0, part(i)], relay.at[0, part(i)], z_next) for i in two]
     t_far_passed = [copy(T_FAR_PASSED + i, relay.at[0, part(i)], tx.at[2, part(i)], y_next2) for i in two]
+    t_direct = [copy(T_DIRECT + i, tx.at[0, part(i)], tx.at[2, part(i)], next2_dev) for i in two]
     t_hop = [copy(T_HOP + i, tx.at[1, part(i)], tx.at[1, side_part(i)], side_dev) for i in two]
     t_far = [copy(T_FAR + i, tx.at[1, part(i)], tx.at[2, part(i)], next_dev) for i in two]
     t_far_hop = [copy(T_FAR_HOP + i, tx.at[2, part(i)], tx.at[2, side_part(i)], side_dev) for i in two]
@@ -176,6 +183,7 @@
     ]
     ig_za = [copy(IG_AZ + i, img_out.at[2, part(i)], img_in.at[2, part(i)], z_dev) for i in two]
     free = jnp.logical_not(crowded)
+    crowded_back = first | last
 
     for i in later:
         pl.when(by_z[i])(t_relay[i].start)
@@ -186,6 +194,7 @@
             t_next[i].start()
     for i in two:
         pl.when(before & (c == 1))(t_far_z[i].start)
+        pl.when(last & (c == 1))(t_direct[i].start)
     early, late = two[:HALF], two[HALF:]
     for i, k in zip(early, late):
         img_z[i].start()
@@ -219,14 +228,15 @@
             if i == later[0]:
                 pl.when(last & jnp.logical_not(lowest))(pass_relayed)
             t_next[i].wait_recv()
-            pl.when((c == 1) & jnp.logical_not(last))(t_far[i].start)
+            pl.when((c == 1) & jnp.logical_not(last | first))(t_far[i].start)
             t_hop[i].start()
         pl.when(before & jnp.logical_not(lowest) & (c == 1))(pass_far_relayed)
 
     def pass_far():
         for i in two:
             pl.when(first)(t_far_passed[i].wait_recv)
-            pl.when(jnp.logical_not(first))(t_far[i].wait_recv)
+            pl.when(second)(t_direct[i].wait_recv)
+            pl.when(jnp.logical_not(first | second))(t_far[i].wait_recv)
             t_far_hop[i].start()
 
     for i, k in zip(early, late):
@@ -263,18 +273,20 @@
     pl.when(before & lowest & (c == 1))(pass_far_relayed)
     t_side.wait_recv()
 
+    wait = jnp.where(first & (c == 0), 1, 0)
+
     def tile(s, _):
-        j = (s + 1) // 2 - (s // 3) * (2 - 2 * c)
-        other = s // 2
+        j = wait * (s // 2) + (1 - wait) * ((s + 1) // 2 - (s // 3) * (2 - 2 * c))
+        other = wait * (s % 2) + (1 - wait) * (s // 2)
         i = c + other * (1 - 2 * c)
 
-        @pl.when(s == 1)
-        def _():
-            pl.when((c == 1) & jnp.logical_not(first | second))(pass_far)
+        @pl.when(s == 1 + wait)
+        def _():
+            pl.when((c == 1) & jnp.logical_not(first | (second & lowest)))(pass_far)
             for q in two:
                 t_hop[q].wait_recv()
 
-        @pl.when(s == 2)
+        @pl.when(s == 2 - wait)
         def _():
             for q in range(4):
                 img_got[q].wait_recv()
@@ -286,7 +298,7 @@
 
         @pl.when((s == 3) & (c == 1))
         def _():
-            pl.when(second)(pass_far)
+            pl.when(second & lowest)(pass_far)
             for q in two:
                 t_far_hop[q].wait_recv()
 
@@ -305,7 +317,7 @@
             side_out[...] = tg[0, side].astype(BF16)
             g_side.start()
 
-        @pl.when(s == 2)
+        @pl.when(s == 2 + wait)
         def _():
             for q in two:
                 hop_out[0, part(q)] = tg[1, side_part(q)].astype(BF16)
@@ -333,20 +345,20 @@
         for q in (i, k):
             img_out[2, part(q)] = ready_part(3, q).astype(BF16)
         ig_az[i].start()
-        pl.when(crowded)(ig_az[k].start)
-        pl.when(free)(ig_za[k].start)
+        pl.when(crowded_back)(ig_az[k].start)
+        pl.when(jnp.logical_not(crowded_back))(ig_za[k].start)
     ig_core[1].wait_recv()
     ig_core[2].wait_recv()
     for i, k in zip(early, late):
         img_out[0, part(i)] = ready_part(1, i).astype(BF16)
         ig_a[i].start()
 
-        @pl.when(free)
+        @pl.when(jnp.logical_not(crowded_back))
         def _():
             img_out[1, part(k)] = ready_part(2, k).astype(BF16)
             ig_z[k].start()
 
-        @pl.when(crowded)
+        @pl.when(crowded_back)
         def _():
             img_out[0, part(k)] = ready_part(1, k).astype(BF16)
             ig_a[k].start()
@@ -391,12 +403,12 @@
         far_back(2 * i + 1)
         ig_az[k].wait_recv()
 
-        @pl.when(free)
+        @pl.when(jnp.logical_not(crowded_back))
         def _():
             img_out[0, part(k)] = (ready_part(1, k) + img_in[2, part(k)].astype(F32)).astype(BF16)
             ig_a[k].start()
 
-        @pl.when(crowded)
+        @pl.when(crowded_back)
         def _():
             img_out[1, part(k)] = (ready_part(2, k) + img_in[2, part(k)].astype(F32)).astype(BF16)
             ig_z[k].start()
@@ -411,7 +423,8 @@
         for sent in (*t_far_hop, *g_far_hop):
             sent.wait_send()
         for i in two:
-            pl.when(jnp.logical_not(last))(t_far[i].wait_send)
+            pl.when(jnp.logical_not(last | first))(t_far[i].wait_send)
+            pl.when(last)(t_direct[i].wait_send)
             pl.when(before)(t_far_z[i].wait_send)
             pl.when(before)(t_far_passed[i].wait_send)
 
@@ -472,13 +485,13 @@
 
 
 def hand_over(image_ref, text_ref, image_out, text_out, held, load_sem, store_sem):
-    half = image_ref.shape[0] // 2
-    pieces = [(n, i) for n in range(2) for i in range(2)]
+    half = image_ref.shape[0] // 4
+    pieces = [(n, i) for n in range(2) for i in range(4)]
     loads, stores = [], []
     for n, i in pieces:
         rows = pl.ds(i * half, half)
         source, target = (image_ref, image_out) if n == 0 else (text_ref, text_out)
-        k = 2 * n + i
+        k = 4 * n + i
         loads.append(pltpu.make_async_copy(source.at[rows], held.at[k], load_sem.at[k]))
         stores.append(pltpu.make_async_copy(held.at[k], target.at[rows], store_sem.at[k]))
     for load in loads:
@@ -541,9 +554,9 @@
             in_specs=[anywhere] * 2,
             out_specs=(anywhere,) * 2,
             scratch_shapes=[
-                pltpu.VMEM((4, rows // 2, width), BF16),
-                pltpu.SemaphoreType.DMA((4,)),
-                pltpu.SemaphoreType.DMA((4,)),
+                pltpu.VMEM((8, rows // 4, width), BF16),
+                pltpu.SemaphoreType.DMA((8,)),
+                pltpu.SemaphoreType.DMA((8,)),
             ],
             compiler_params=pltpu.CompilerParams(vmem_limit_bytes=60 * 2**20),
             name="hand_over",

time: 50.1 us -> 49.2 us (0.982)
  the two profiles are of different devices: /device:TPU:1 before, /device:TPU:121 now
where the time goes in v6:
time: 49.2 us; the launch traced here: 49 us
  Pallas kernels  47.7 us (97%)
  between operations  1.29 us (3%)
    pallas_call x1, Pallas kernels, per_device(): pl.pallas_call(functools.partial(kernel, n_blk), out_shape=(jax.ShapeDtyp...  46 us
    pallas_call x1, Pallas kernels, per_device(): pl.pallas_call(hand_over, out_shape=(jax.ShapeDtypeStruct((rows, width),...  1.73 us

profile of v6, /device:TPU:121, one launch (start us, length us, event | category | flops | bytes accessed | tf_op | source)
XLA Modules:
  0.0 49.0 jit_solution(499153538446681176)
XLA Ops:
  1.3 46.0 %window_loss_grad.1 = (bf16[128,768]{1,0:T(8,128)(2,1)}, bf16[128,768]{1,0:T(8,128)(2,1)}) custom-call(f32[1,1]{1,0:T(1,128)} %bitcast.4.scale_ref, bf16[128,768]{1,0:T(8,128)(2,1)} %image_ref.1, bf16[128,768]{1,0:T(8,128)(2,1)} %text_ref.1, f32[1,128]{1,0:T(1,128)} %bitcast.5, f32[1,128]{1,0:T(1,128)} %bitcast.6, s32[1,128]{1,0:T(1,128)} %bitcast.7), custom_call_target="tpu_custom_call" | custom-call | tf_op jit(solution)/shard_map/window_loss_grad/pallas_call | solution.py:512
  47.3 1.7 %hand_over.1 = (bf16[128,768]{1,0:T(8,128)(2,1)}, bf16[128,768]{1,0:T(8,128)(2,1)}) custom-call(bf16[128,768]{1,0:T(8,128)(2,1)} %get-tuple-element.4.image_ref, bf16[128,768]{1,0:T(8,128)(2,1)} %get-tuple-element.5.text_ref), custom_call_target="tpu_custom_call" | custom-call | tf_op jit(solution)/shard_map/hand_over/pallas_call | solution.py:551

commit v7 on v6

--- a/solution.py
+++ b/solution.py
@@ -413,6 +413,18 @@
             img_out[1, part(k)] = (ready_part(2, k) + img_in[2, part(k)].astype(F32)).astype(BF16)
             ig_z[k].start()
 
+    @pl.when(first)
+    def _():
+        for i in back_later:
+            g_relay[i].wait_recv()
+            g_passed[i].start()
+
+    @pl.when(second & (c == 1))
+    def _():
+        for i in two:
+            g_far_z[i].wait_recv()
+            g_far_passed[i].start()
+
     for sent in (t_side, *t_next, *t_hop, *img_a, *img_z, *img_az, *params, *img_core, prm_core, g_side, *g_hop, *ig_core):
         sent.wait_send()
     for i in later:
@@ -427,18 +439,6 @@
             pl.when(last)(t_direct[i].wait_send)
             pl.when(before)(t_far_z[i].wait_send)
             pl.when(before)(t_far_passed[i].wait_send)
-
-    @pl.when(first)
-    def _():
-        for i in back_later:
-            g_relay[i].wait_recv()
-            g_passed[i].start()
-
-    @pl.when(second & (c == 1))
-    def _():
-        for i in two:
-            g_far_z[i].wait_recv()
-            g_far_passed[i].start()
 
     ig_core[0].wait_recv()
     ig[c, own] += core_in[own].astype(F32)

time: 49.2 us -> 49.2 us (level)
  no operation moved by 1% of the time
where the time goes in v7:
time: 49.2 us; the launch traced here: 49 us
  Pallas kernels  47.7 us (97%)
  between operations  1.29 us (3%)
    pallas_call x1, Pallas kernels, per_device(): pl.pallas_call(functools.partial(kernel, n_blk), out_shape=(jax.ShapeDtyp...  46 us
    pallas_call x1, Pallas kernels, per_device(): pl.pallas_call(hand_over, out_shape=(jax.ShapeDtypeStruct((rows, width),...  1.73 us

profile of v7, /device:TPU:121, one launch (start us, length us, event | category | flops | bytes accessed | tf_op | source)
XLA Modules:
  0.0 49.0 jit_solution(8774363675666441338)
XLA Ops:
  1.3 46.0 %window_loss_grad.1 = (bf16[128,768]{1,0:T(8,128)(2,1)}, bf16[128,768]{1,0:T(8,128)(2,1)}) custom-call(f32[1,1]{1,0:T(1,128)} %bitcast.4.scale_ref, bf16[128,768]{1,0:T(8,128)(2,1)} %image_ref.1, bf16[128,768]{1,0:T(8,128)(2,1)} %text_ref.1, f32[1,128]{1,0:T(1,128)} %bitcast.5, f32[1,128]{1,0:T(1,128)} %bitcast.6, s32[1,128]{1,0:T(1,128)} %bitcast.7), custom_call_target="tpu_custom_call" | custom-call | tf_op jit(solution)/shard_map/window_loss_grad/pallas_call | solution.py:512
  47.3 1.7 %hand_over.1 = (bf16[128,768]{1,0:T(8,128)(2,1)}, bf16[128,768]{1,0:T(8,128)(2,1)}) custom-call(bf16[128,768]{1,0:T(8,128)(2,1)} %get-tuple-element.4.image_ref, bf16[128,768]{1,0:T(8,128)(2,1)} %get-tuple-element.5.text_ref), custom_call_target="tpu_custom_call" | custom-call | tf_op jit(solution)/shard_map/hand_over/pallas_call | solution.py:551
